TPU v7x, 1024 devices: a whole 4x8x16 slice. The times are simulated.
1024 devices in a mesh: cap: 64 (over z_hi, y, x), vid: 16 (over z_lo, core).
Axes of the slice: x: 4, y: 8, z: 16 (z_hi: 2, z_lo: 8; z = z_hi * 8 + z_lo), core: 2. Of those that a mesh axis runs over, the one named last changes fastest.
Arguments:
- caption_tokens: bfloat16 [1024, 32, 128], P(('cap', 'vid')), may hold values from -12.1875 to 12.1875
- video_tokens: bfloat16 [1024, 128, 128], P(('cap', 'vid')), may hold values from -0.4875 to 0.4875
- row_norms: bfloat16 [1024], P(('cap', 'vid')), may hold values from 1 to 64, as said below
- col_norms: bfloat16 [1024], P(('cap', 'vid')), may hold values from 1 to 64, as said below
Outputs:
- caption_grads: bfloat16 [1024, 32, 128], P(('cap', 'vid'))
- video_grads: bfloat16 [1024, 128, 128], P(('cap', 'vid'))
Inputs may be any that keep to these rules, and one draw needn't show every extreme that they name: `row_norms`: saved caption normalizers. `col_norms`: saved video normalizers.
All inputs are finite; a program needn't handle non-finite values.
Results may differ from a plain program's by a relative error of at most 0.015.
Values may be sent and summed in bfloat16 or wider, within the bound.
No kernel may reach another device: no remote copies, remote signals or barrier semaphores. Data moves between devices by JAX's collectives and lax.ppermute only.
A program may use at most 128 MiB of HBM per device.

v0:
```python
import math

import jax
import jax.numpy as jnp
from jax import lax
from jax.sharding import PartitionSpec as P

pool_tau = 0.05
logit_temp = 0.5


def block_grads(captions, caption_norm, caption_ids, videos, video_norm, video_ids):
    cap_rows, cap_len, features = captions.shape
    vid_rows, vid_len, _ = videos.shape
    group_size = math.gcd(8, vid_rows)
    group_count = vid_rows // group_size
    queries = captions.reshape(cap_rows * cap_len, features)
    row_norm = caption_norm.astype(jnp.float32)
    key_groups = videos.reshape(group_count, group_size * vid_len, features)
    norm_groups = video_norm.astype(jnp.float32).reshape(group_count, group_size)
    id_groups = video_ids.reshape(group_count, group_size)

    def advance(query_total, pieces):
        key_rows, col_norm, col_ids = pieces
        scores = (
            lax.dot_general(
                queries, key_rows, (((1,), (1,)), ((), ())), preferred_element_type=jnp.float32
            )
            / pool_tau
        )
        scores = scores.reshape(cap_rows, cap_len, group_size, vid_len)
        row_peak = jnp.max(scores, axis=3, keepdims=True)
        lifted = jnp.exp(scores - row_peak)
        summed = jnp.sum(lifted, axis=3, keepdims=True)
        weights = lifted / summed
        pooled = pool_tau * (row_peak[..., 0] + jnp.log(summed[..., 0]))
        logits = jnp.mean(pooled, axis=1) / logit_temp
        positive = (caption_ids[:, None] == col_ids[None, :]).astype(jnp.float32)
        pair_grad = (
            jnp.exp(logits - row_norm[:, None])
            + jnp.exp(logits - col_norm[None, :])
            - 2.0 * positive
        ) / (2.0 * logit_temp)
        token_coef = (pair_grad[:, None, :, None] * weights / cap_len).astype(jnp.bfloat16)
        token_coef = token_coef.reshape(cap_rows * cap_len, group_size * vid_len)
        query_total = query_total + jnp.dot(
            token_coef, key_rows, preferred_element_type=jnp.float32
        )
        key_part = lax.dot_general(
            token_coef, queries, (((0,), (0,)), ((), ())), preferred_element_type=jnp.float32
        )
        return (query_total, key_part)

    start_total = jnp.zeros((cap_rows * cap_len, features), jnp.float32)
    query_total, key_parts = lax.scan(advance, start_total, (key_groups, norm_groups, id_groups))
    return (
        query_total.reshape(cap_rows, cap_len, features),
        key_parts.reshape(vid_rows, vid_len, features),
    )


def local(caption_tokens, video_tokens, row_norms, col_norms):
    cap_count = lax.axis_size("cap")
    vid_count = lax.axis_size("vid")
    pair_count = caption_tokens.shape[0]
    cap_index = lax.axis_index("cap")
    vid_index = lax.axis_index("vid")
    offsets = jnp.arange(pair_count, dtype=jnp.int32)
    captions, caption_norm = (
        lax.all_gather(caption_tokens, "vid", axis=0, tiled=True),
        lax.all_gather(row_norms, "vid", axis=0, tiled=True),
    )
    videos, video_norm = (
        lax.all_gather(video_tokens, "cap", axis=0, tiled=True),
        lax.all_gather(col_norms, "cap", axis=0, tiled=True),
    )
    block_caps = cap_index * vid_count + jnp.arange(vid_count, dtype=jnp.int32)
    block_vids = jnp.arange(cap_count, dtype=jnp.int32) * vid_count + vid_index
    caption_ids = (block_caps[:, None] * pair_count + offsets[None, :]).reshape(-1)
    video_ids = (block_vids[:, None] * pair_count + offsets[None, :]).reshape(-1)
    query_part, key_part = block_grads(
        captions, caption_norm, caption_ids, videos, video_norm, video_ids
    )
    caption_grads = lax.psum_scatter(query_part, "vid", scatter_dimension=0, tiled=True)
    video_grads = lax.psum_scatter(key_part, "cap", scatter_dimension=0, tiled=True)
    return (caption_grads.astype(jnp.bfloat16), video_grads.astype(jnp.bfloat16))


def solution(mesh):
    return jax.shard_map(
        local,
        mesh=mesh,
        in_specs=(
            P(("cap", "vid"), None, None),
            P(("cap", "vid"), None, None),
            P(("cap", "vid")),
            P(("cap", "vid")),
        ),
        out_specs=(P(("cap", "vid"), None, None), P(("cap", "vid"), None, None)),
        check_vma=False,
    )
```

profile of v0, /device:TPU:64, one launch (start us, length us, event | category | flops | bytes accessed | tf_op | source)
XLA Modules:
  0.0 1372.1 jit_solution(12702587975670712173)
XLA Ops:
  10.6 50.2 %all-reduce = bf16[16]{0:T(256)(128)(2,1)S(1)} all-reduce(bf16[16]{0:T(256)(128)(2,1)S(1)} %dynamic-update-slice), channel_id=1, replica_groups=mesh['cap'=64,'vid'=16] {'vid'}, use_global_device_ids=true, to_apply=%add | all-reduce | flops 16 | bytes 64
  63.5 312.0 %all-reduce.1 = bf16[64]{0:T(256)(128)(2,1)S(1)} all-reduce(bf16[64]{0:T(256)(128)(2,1)S(1)} %dynamic-update-slice.1), channel_id=1, replica_groups=mesh['cap'=64,'vid'=16] {'cap'}, use_global_device_ids=true, to_apply=%add.1 | all-reduce | flops 64 | bytes 256
  375.6 33.9 %all_gather.13 = bf16[16,32,128]{2,1,0:T(8,128)(2,1)S(1)} all-gather(bf16[1,32,128]{2,1,0:T(8,128)(2,1)} %param.6), channel_id=1, replica_groups=mesh['cap'=64,'vid'=16] {'vid'}, dimensions={0}, use_global_device_ids=true | all-gather | bytes 139264 | tf_op jit(solution)/shard_map/all_gather | solution.py:70
  409.5 237.4 %while.15 = (s32[]{:T(128)}, f32[512,128]{1,0:T(8,128)S(1)}, f32[8,1024,128]{2,1,0:T(8,128)}, bf16[8,1024,128]{2,1,0:T(8,128)(2,1)}, bf16[512,128]{1,0:T(8,128)(...) while((s32[]{:T(128)}, f32[512,128]{1,0:T(8,128)S(1)}, ...), condition=%wide.region_4.5_spmd.clone, body=%wide.region_0.4_spmd.clone.sunk | while | flops 407507712 | bytes 59625472 | solution.py:55
  410.9 1.8 copy.32
  412.8 2.1 copy.33
  417.2 1.9 copy.34
  419.1 2.9 copy.35
  424.4 3.0 copy.37
  427.9 1.8 copy.38
  429.8 2.9 copy.39
  432.6 3.9 multiply_convert_fusion.2
  440.6 1.8 copy.32
  442.4 2.1 copy.33
  446.9 1.9 copy.34
  448.7 2.9 copy.35
  454.0 3.0 copy.37
  457.6 1.8 copy.38
  459.4 2.9 copy.39
  462.3 3.9 multiply_convert_fusion.2
  470.3 1.8 copy.32
  472.1 2.1 copy.33
  476.6 1.9 copy.34
  478.4 2.9 copy.35
  483.7 3.0 copy.37
  489.1 2.9 copy.39
  492.0 3.9 multiply_convert_fusion.2
  500.0 1.8 copy.32
  501.8 2.1 copy.33
  506.3 1.9 copy.34
  508.1 2.9 copy.35
  513.4 3.0 copy.37
  518.8 2.9 copy.39
  521.7 3.9 multiply_convert_fusion.2
  529.6 1.8 copy.32
  531.5 2.1 copy.33
  535.9 1.9 copy.34
  537.8 2.9 copy.35
  543.1 3.0 copy.37
  548.5 2.9 copy.39
  551.3 3.9 multiply_convert_fusion.2
  559.3 1.8 copy.32
  561.1 2.1 copy.33
  565.6 1.9 copy.34
  567.5 2.9 copy.35
  572.7 3.0 copy.37
  578.1 2.9 copy.39
  581.0 3.9 multiply_convert_fusion.2
  589.0 1.8 copy.32
  590.8 2.1 copy.33
  595.3 1.9 copy.34
  597.2 2.9 copy.35
  602.4 3.0 copy.37
  607.8 2.9 copy.39
  610.7 3.9 multiply_convert_fusion.2
  618.6 1.8 copy.32
  620.5 2.1 copy.33
  625.0 1.9 copy.34
  626.8 2.9 copy.35
  632.1 3.0 copy.37
  637.5 2.9 copy.39
  640.4 3.9 multiply_convert_fusion.2
  648.4 93.1 %reduce-scatter.3.cloned.1.call-done = f32[1,32,128]{2,1,0:T(8,128)} async-done(((f32[16,32,128]{2,1,0:T(8,128)}), f32[1,32,128]{2,1,0:T(8,128)}) %reduce-scatter.3.cloned.1.call-update) | async-done | bytes 16400 | tf_op jit(solution)/shard_map/reduce_scatter | solution.py:84
  742.8 621.3 %reduce-scatter.5.cloned.1.call-done = f32[1,128,128]{2,1,0:T(8,128)} async-done(((f32[64,128,128]{2,1,0:T(8,128)}), f32[1,128,128]{2,1,0:T(8,128)}) %reduce-scatter.5.cloned.1.call-update) | async-done | bytes 65552 | tf_op jit(solution)/shard_map/reduce_scatter | solution.py:85
  (140 shorter events, 95.2 us)
Async XLA Ops:
  7.2 402.4 %all-gather.2.cloned.1.call-start = ((), (), s32[]{:S(2)}) async-start(), calls=%async_computation.2 | async-start | bytes 2129920 | tf_op jit(solution)/shard_map/all_gather | solution.py:74
  7.9 733.5 %reduce-scatter.3.cloned.1.call-start = ((), (), s32[]{:S(2)}) async-start(), calls=%async_computation.3 | async-start | bytes 278528 | tf_op jit(solution)/shard_map/reduce_scatter | solution.py:84
  646.9 0.7 copy-start
  647.6 716.4 %reduce-scatter.5.cloned.1.call-start = ((), (), s32[]{:S(2)}) async-start(), calls=%async_computation.4 | async-start | bytes 4259840 | tf_op jit(solution)/shard_map/reduce_scatter | solution.py:85
Sparse Core Ops, SparseCore 0:
  13.8 186.1 all-gather.1
  647.8 93.6 reduce-scatter.2
  745.2 618.8 reduce-scatter.4
where the time goes:
time: 1370 us
  waiting for transfers between devices  716 us (52%)
  blocking collectives  396 us (29%)
  local copies, waits for them, and re-layouts  161 us (12%)
  other arithmetic  50.6 us (4%)
  matrix products  32.7 us (2%)
  between operations  15.1 us (1%)
    reduce_scatter x1, waiting for transfers between devices, local(): lax.psum_scatter(key_part, 'cap', scatter_dimension=0, tiled=True)  621 us
    unnamed x2, blocking collectives  362 us
    reduce_scatter x1, waiting for transfers between devices, local(): lax.psum_scatter(query_part, 'vid', scatter_dimension=0, tiled=True)  93.1 us
    while x32, local copies, waits for them, and re-layouts  60 us
    all_gather x1, blocking collectives, local(): lax.all_gather(caption_tokens, 'vid', axis=0, tiled=True)  33.9 us
    convert_element_type x8, other arithmetic, advance(): (pair_grad[:, None, :, None] * weights / cap_len).astype(jnp.bfloat16)  30.9 us
    div x16, local copies, waits for them, and re-layouts, advance(): weights = lifted / summed  28.4 us
    sub x16, local copies, waits for them, and re-layouts, advance(): lifted = jnp.exp(scores - row_peak)  27.8 us
  transfers between devices with their start and end apart: 3, of which 2 were waited for; matrix products, arithmetic and copies ran while one was open for 0% of the time, Pallas kernels for 0%

commit v1 on v0

v1 whole, which is shorter than its diff:
```python
import functools
import math

import jax
import jax.numpy as jnp
from jax import lax
from jax.experimental import pallas as pl
from jax.experimental.pallas import tpu as pltpu
from jax.sharding import Mesh
from jax.sharding import PartitionSpec as P

pool_tau = 0.05
logit_temp = 0.5


def pair_kernel(
    caps_ref, vids_ref, dq_ref, dv_ref, own_dq_ref, own_dv_ref,
    lift_ref, coef_ref, peak_ref, sum_ref, turned_ref, total_ref, mine_ref, *, q_len, v_len, lanes,
):
    cap_rows, vid_rows = caps_ref.shape[0], vids_ref.shape[0]
    features = caps_ref.shape[2]
    block_caps = lanes // q_len
    blocks = cap_rows // block_caps
    to_exp2 = 1.0 / (pool_tau * math.log(2.0))

    own_cap = lax.axis_index("x") * lax.axis_size(Z) + lax.axis_index("z_hi") * lax.axis_size("z_lo") + lax.axis_index("z_lo")
    own_vid = lax.axis_index("core") * lax.axis_size("y") + lax.axis_index("y")
    cap_bits = block_caps.bit_length() - 1
    own_block, own_place = own_cap >> cap_bits, own_cap & (block_caps - 1)

    turned_ref[...] = vids_ref[:, :v_len, :].reshape(vid_rows * v_len, features).T
    total_ref[...] = jnp.zeros_like(total_ref)

    def queries_of(block):
        return caps_ref[pl.ds(block * block_caps, block_caps), :q_len, :].reshape(lanes, features)

    @pl.loop(0, blocks)
    def _(block):
        queries = queries_of(block)
        for v in range(vid_rows):
            scores = lax.dot_general(
                vids_ref[v, :v_len, :], queries, (((1,), (1,)), ((), ())), preferred_element_type=jnp.float32
            )
            peak = jnp.max(scores, axis=0, keepdims=True)
            lifted = jnp.exp2((scores - peak) * to_exp2)
            lift_ref[block, v] = lifted
            peak_ref[block, pl.ds(v, 1), :] = peak
            sum_ref[block, pl.ds(v, 1), :] = jnp.sum(lifted, axis=0, keepdims=True)

    q_bits = q_len.bit_length() - 1
    row = lax.broadcasted_iota(jnp.int32, (lanes, lanes), 0) >> q_bits
    col = lax.broadcasted_iota(jnp.int32, (lanes, lanes), 1) >> q_bits
    spread = jnp.where(row == col, 1.0 / (q_len * logit_temp), 0.0)
    col_norm = vids_ref[:, v_len, :1].astype(jnp.float32)
    lane_cap = lax.broadcasted_iota(jnp.int32, (vid_rows, lanes), 1) >> q_bits
    sub_vid = lax.broadcasted_iota(jnp.int32, (vid_rows, lanes), 0)

    mine_ref[...] = jnp.zeros_like(mine_ref)

    @pl.loop(0, blocks)
    def _(block):
        summed = sum_ref[block]
        pooled = peak_ref[block] + pool_tau * jnp.log(summed)
        logits = jnp.dot(pooled, spread, preferred_element_type=jnp.float32, precision=lax.Precision.HIGHEST)
        row_norm = jnp.zeros((1, lanes), jnp.float32)
        for c in range(block_caps):
            norm = caps_ref[block * block_caps + c, pl.ds(q_len, 1), :].astype(jnp.float32)
            norm = jnp.concatenate([norm] * (lanes // norm.shape[1]), axis=1)
            row_norm = jnp.where(lane_cap[:1] == c, norm, row_norm)
        paired = (lane_cap + block * block_caps == own_cap) & (sub_vid == own_vid)
        pair_grad = (jnp.exp(logits - row_norm) + jnp.exp(logits - col_norm) - 2.0 * paired.astype(jnp.float32)) / (2.0 * logit_temp)
        scale = pair_grad / (summed * q_len)
        sum_ref[block] = jnp.where(paired, 0.0, scale)
        mine_ref[...] += jnp.where(paired, scale, 0.0)

    @pl.loop(0, blocks)
    def _(block):
        queries = queries_of(block)
        for v in range(vid_rows):
            coef_ref[pl.ds(v * v_len, v_len), :] = (lift_ref[block, v] * sum_ref[block, pl.ds(v, 1), :]).astype(jnp.bfloat16)
        coef = coef_ref[...]
        turned = jnp.dot(turned_ref[...], coef, preferred_element_type=jnp.float32)
        dq_ref[pl.ds(block * block_caps, block_caps)] = turned.T.reshape(block_caps, q_len, features).astype(dq_ref.dtype)
        total_ref[...] += jnp.dot(coef, queries, preferred_element_type=jnp.float32)

    dv_ref[...] = total_ref[...].reshape(dv_ref.shape).astype(dv_ref.dtype)

    own_scale = jnp.sum(mine_ref[...], axis=0, keepdims=True)
    coef = (lift_ref[own_block, own_vid] * own_scale).astype(jnp.bfloat16)
    own_dv_ref[...] = jnp.dot(coef, queries_of(own_block), preferred_element_type=jnp.float32)
    total_ref[pl.ds(0, lanes), :] = lax.dot_general(
        coef, vids_ref[own_vid, :v_len, :], (((0,), (0,)), ((), ())), preferred_element_type=jnp.float32
    )
    own_dq_ref[...] = total_ref[pl.ds(own_place * q_len, q_len), :]


def pair_grads(caps, vids, q_len, v_len, lanes=256):
    cap_rows, vid_rows, features = caps.shape[0], vids.shape[0], caps.shape[2]
    blocks = cap_rows * q_len // lanes
    return pl.pallas_call(
        functools.partial(pair_kernel, q_len=q_len, v_len=v_len, lanes=lanes),
        out_shape=(
            jax.ShapeDtypeStruct((cap_rows, q_len, features), jnp.bfloat16),
            jax.ShapeDtypeStruct((vid_rows, v_len, features), jnp.bfloat16),
            jax.ShapeDtypeStruct((q_len, features), jnp.float32),
            jax.ShapeDtypeStruct((v_len, features), jnp.float32),
        ),
        in_specs=[
            pl.BlockSpec(memory_space=pltpu.VMEM),
            pl.BlockSpec(memory_space=pltpu.VMEM),
        ],
        out_specs=[pl.BlockSpec(memory_space=pltpu.VMEM)] * 4,
        scratch_shapes=[
            pltpu.VMEM((blocks, vid_rows, v_len, lanes), jnp.float32),
            pltpu.VMEM((vid_rows * v_len, lanes), jnp.bfloat16),
            pltpu.VMEM((blocks, vid_rows, lanes), jnp.float32),
            pltpu.VMEM((blocks, vid_rows, lanes), jnp.float32),
            pltpu.VMEM((features, vid_rows * v_len), jnp.bfloat16),
            pltpu.VMEM((vid_rows * v_len, features), jnp.float32),
            pltpu.VMEM((vid_rows, lanes), jnp.float32),
        ],
        compiler_params=pltpu.CompilerParams(vmem_limit_bytes=48 * 2**20),
        cost_estimate=pl.CostEstimate(
            flops=6 * cap_rows * q_len * vid_rows * v_len * features,
            bytes_accessed=4 * (cap_rows * q_len + vid_rows * v_len) * features,
            transcendentals=cap_rows * q_len * vid_rows * v_len,
        ),
    )(caps, vids)


PARTS = (2, 8, 4, 8, 2)
AXES = ("z_hi", "y", "x", "z_lo", "core")
Z = ("z_hi", "z_lo")


def with_norm(tokens, norm):
    return jnp.concatenate([tokens, jnp.broadcast_to(norm[:, None, None], (1, 8, tokens.shape[2]))], axis=1)


def spread_over(block, axis):
    size = lax.axis_size(axis)
    copies = jnp.broadcast_to(block[None], (size, *block.shape))
    return lax.all_to_all(copies, axis, 0, 0, tiled=True)


def sum_over(parts, axis):
    moved = lax.all_to_all(parts, axis, 0, 0, tiled=True)
    return jnp.sum(moved.astype(jnp.float32), axis=0)


def local(caption_tokens, video_tokens, row_norms, col_norms):
    q_len, v_len, features = caption_tokens.shape[1], video_tokens.shape[1], caption_tokens.shape[2]
    x_count, y_count, z_count = lax.axis_size("x"), lax.axis_size("y"), lax.axis_size(Z)
    caps = spread_over(with_norm(caption_tokens, row_norms)[0], Z)
    caps = spread_over(caps, "x").reshape(x_count * z_count, q_len + 8, features)
    vids = spread_over(with_norm(video_tokens, col_norms)[0], "y")
    vids = lax.all_gather(vids, "core", axis=0, tiled=True)
    dq, dv, own_dq, own_dv = pair_grads(caps, vids, q_len, v_len)
    dv = sum_over(dv.reshape(-1, y_count, v_len, features), "core").astype(jnp.bfloat16)
    dv = (sum_over(dv, "y") + own_dv).astype(jnp.bfloat16)
    dq = sum_over(dq.reshape(x_count, z_count, q_len, features), "x").astype(jnp.bfloat16)
    dq = (sum_over(dq, Z) + own_dq).astype(jnp.bfloat16)
    return dq[None], dv[None]


def solution(mesh):
    fine = Mesh(mesh.devices.reshape(PARTS), AXES)
    return jax.shard_map(
        local,
        mesh=fine,
        in_specs=(P(AXES, None, None), P(AXES, None, None), P(AXES), P(AXES)),
        out_specs=(P(AXES, None, None), P(AXES, None, None)),
        check_vma=False,
    )
```

time: 1370 us -> 133 us (0.10)
  the two profiles are of different devices: /device:TPU:64 before, /device:TPU:2 now
where the time goes in v1:
time: 133 us; the launch traced here: 132 us
  waiting for transfers between devices  47.8 us (36%)
  blocking collectives  39.6 us (30%)
  starting transfers between devices  24.3 us (18%)
  Pallas kernels  13.2 us (10%)
  other arithmetic  2.86 us (2%)
  local copies, waits for them, and re-layouts  2.47 us (2%)
  between operations  2 us (2%)
    all_to_all x1, blocking collectives, spread_over(): return lax.all_to_all(copies, axis, 0, 0, tiled=True)  33.2 us
    all_to_all x3, waiting for transfers between devices, sum_over(): moved = lax.all_to_all(parts, axis, 0, 0, tiled=True)  31.2 us
    all_to_all x2, waiting for transfers between devices, spread_over(): return lax.all_to_all(copies, axis, 0, 0, tiled=True)  16.7 us
    pallas_call x1, Pallas kernels, pair_grads(): pl.pallas_call(functools.partial(pair_kernel, q_len=q_len, v_len=v_len, l...  13.2 us
    all_to_all x3, starting transfers between devices, sum_over(): moved = lax.all_to_all(parts, axis, 0, 0, tiled=True)  12.3 us
    all_to_all x2, starting transfers between devices, spread_over(): return lax.all_to_all(copies, axis, 0, 0, tiled=True)  12.1 us
    all_to_all x1, blocking collectives, sum_over(): moved = lax.all_to_all(parts, axis, 0, 0, tiled=True)  4.14 us
  transfers between devices with their start and end apart: 5, of which 5 were waited for; matrix products, arithmetic and copies ran while one was open for 2% of the time, Pallas kernels for 0%

profile of v1, /device:TPU:2, one launch (start us, length us, event | category | flops | bytes accessed | tf_op | source)
XLA Modules:
  0.0 132.2 jit_solution(7311624859984351709)
XLA Ops:
  1.3 0.8 pad_bitcast_fusion
  2.0 0.7 broadcast_in_dim.44
  2.8 0.0 copy-start
  2.8 7.2 %all-to-all-start.2 = ((bf16[8,136,128]{2,1,0:T(8,128)(2,1)}), bf16[8,136,128]{2,1,0:T(8,128)(2,1)S(1)}, u32[]{:S(2)}, u32[]{:S(2)}) async-start(bf16[8,136,128]{2,1,0:T(8,128)(2,1)} %broadcast_in_dim.44), calls=%async_computation.2 | async-start | bytes 557056 | tf_op jit(solution)/shard_map/all_to_all | solution.py:143
  10.7 0.0 copy-done
  10.7 11.5 %all-to-all-done.2 = bf16[8,136,128]{2,1,0:T(8,128)(2,1)S(1)} async-done(((bf16[8,136,128]{2,1,0:T(8,128)(2,1)}), bf16[8,136,128]{2,1,0:T(8,128)(2,1)S(1)}, u32[]{:S(2)}, u32[]{:S(2)}) %all-to-all-start.2) | async-done | bytes 278560 | tf_op jit(solution)/shard_map/all_to_all | solution.py:143
  22.3 33.2 %all_to_all.35 = bf16[16,40,128]{2,1,0:T(8,128)(2,1)S(1)} all-to-all(bf16[16,40,128]{2,1,0:T(8,128)(2,1)S(1)} %broadcast_in_dim.40), channel_id=1, replica_groups=mesh['z_hi'=2,'y'=8,'x'=4,'z_lo'=8,'core'=2] {'z_hi','z_lo'}, dimensions={0} | all-to-all | bytes 327680 | tf_op jit(solution)/shard_map/all_to_all | solution.py:143
  55.5 0.9 broadcast_in_dim.41
  56.4 4.8 %all-to-all-start.1 = ((bf16[4,16,40,128]{3,2,1,0:T(8,128)(2,1)}), bf16[4,16,40,128]{3,2,1,0:T(8,128)(2,1)S(1)}, u32[]{:S(2)}, u32[]{:S(2)}) async-start(bf16[4,16,40,128]{3,2,1,0:T(8,128)(2,1)} %broadcast_in_dim.41), calls=%async_computation.1 | async-start | bytes 1310720 | tf_op jit(solution)/shard_map/all_to_all | solution.py:143
  61.3 2.2 %all_gather.3.vids_ref = bf16[16,136,128]{2,1,0:T(8,128)(2,1)S(1)} all-gather(bf16[8,136,128]{2,1,0:T(8,128)(2,1)S(1)} %all-to-all-done.2), channel_id=1, replica_groups=mesh['z_hi'=2,'y'=8,'x'=4,'z_lo'=8,'core'=2] {'core'}, dimensions={0}, use_global_device_ids=true | all-gather | bytes 835584 | tf_op jit(solution)/shard_map/all_gather | solution.py:157
  63.5 5.1 %all-to-all-done.1 = bf16[4,16,40,128]{3,2,1,0:T(8,128)(2,1)S(1)} async-done(((bf16[4,16,40,128]{3,2,1,0:T(8,128)(2,1)}), bf16[4,16,40,128]{3,2,1,0:T(8,128)(2,1)S(1)}, u32[]{:S(2)}, u32[]{:S(2)}) %all-to-all-start.1) | async-done | bytes 655392 | tf_op jit(solution)/shard_map/all_to_all | solution.py:143
  68.6 13.2 %shard_map.59 = (bf16[64,32,128]{2,1,0:T(8,128)(2,1)}, bf16[16,128,128]{2,1,0:T(8,128)(2,1)S(1)}, f32[32,128]{1,0:T(8,128)S(1)}, f32[128,128]{1,0:T(8,128)S(1)}) custom-call(bf16[64,40,128]{2,1,0:T(8,128)(2,1)S(1)} %bitcast.15, bf16[16,136,128]{2,1,0:T(8,128)(2,1)S(1)} %all_gather.3.vids_ref), custom_call_target="tpu_custom_call" | custom-call | flops 3221225472 | bytes 2097152 | tf_op jit(solution)/shard_map/pallas_call | solution.py:100
  81.8 4.1 %all_to_all.36 = bf16[2,8,128,128]{3,2,1,0:T(8,128)(2,1)S(1)} all-to-all(bf16[2,8,128,128]{3,2,1,0:T(8,128)(2,1)S(1)} %bitcast.16), channel_id=1, replica_groups=mesh['z_hi'=2,'y'=8,'x'=4,'z_lo'=8,'core'=2] {'core'}, dimensions={0} | all-to-all | bytes 1048576 | tf_op jit(solution)/shard_map/all_to_all | solution.py:147
  85.9 4.9 %all-to-all-start.3 = ((bf16[4,16,32,128]{3,2,1,0:T(8,128)(2,1)}), bf16[4,16,32,128]{3,2,1,0:T(8,128)(2,1)S(1)}, u32[]{:S(2)}, u32[]{:S(2)}) async-start(bf16[4,16,32,128]{3,2,1,0:T(8,128)(2,1)} %bitcast.5), calls=%async_computation.3 | async-start | bytes 1048576 | tf_op jit(solution)/shard_map/all_to_all | solution.py:147
  90.8 0.8 reduce_sum.44
  91.6 7.8 %all-to-all-done.3 = bf16[4,16,32,128]{3,2,1,0:T(8,128)(2,1)S(1)} async-done(((bf16[4,16,32,128]{3,2,1,0:T(8,128)(2,1)}), bf16[4,16,32,128]{3,2,1,0:T(8,128)(2,1)S(1)}, u32[]{:S(2)}, u32[]{:S(2)}) %all-to-all-start.3) | async-done | bytes 524320 | tf_op jit(solution)/shard_map/all_to_all | solution.py:147
  99.4 3.4 %all-to-all-start.6 = ((bf16[8,128,128]{2,1,0:T(8,128)(2,1)}), bf16[8,128,128]{2,1,0:T(8,128)(2,1)S(1)}, u32[]{:S(2)}, u32[]{:S(2)}) async-start(bf16[8,128,128]{2,1,0:T(8,128)(2,1)} %reduce_sum.44), calls=%async_computation.6 | async-start | bytes 524288 | tf_op jit(solution)/shard_map/all_to_all | solution.py:147
  102.8 0.7 reduce_sum.42
  103.5 10.8 %all-to-all-done.6 = bf16[8,128,128]{2,1,0:T(8,128)(2,1)S(1)} async-done(((bf16[8,128,128]{2,1,0:T(8,128)(2,1)}), bf16[8,128,128]{2,1,0:T(8,128)(2,1)S(1)}, u32[]{:S(2)}, u32[]{:S(2)}) %all-to-all-start.6) | async-done | bytes 262176 | tf_op jit(solution)/shard_map/all_to_all | solution.py:147
  114.3 4.0 %all-to-all-start.4 = ((bf16[16,32,128]{2,1,0:T(8,128)(2,1)}), bf16[16,32,128]{2,1,0:T(8,128)(2,1)S(1)}, u32[]{:S(2)}, u32[]{:S(2)}) async-start(bf16[16,32,128]{2,1,0:T(8,128)(2,1)} %reduce_sum.42), calls=%async_computation.4 | async-start | bytes 262144 | tf_op jit(solution)/shard_map/all_to_all | solution.py:147
  118.4 0.6 fusion
  119.0 12.6 %all-to-all-done.4 = bf16[16,32,128]{2,1,0:T(8,128)(2,1)S(1)} async-done(((bf16[16,32,128]{2,1,0:T(8,128)(2,1)}), bf16[16,32,128]{2,1,0:T(8,128)(2,1)S(1)}, u32[]{:S(2)}, u32[]{:S(2)}) %all-to-all-start.4) | async-done | bytes 131104 | tf_op jit(solution)/shard_map/all_to_all | solution.py:147
  131.6 0.6 fusion.1
  (4 shorter events, 0.1 us)
Async XLA Ops:
  2.8 7.9 %copy-start = (bf16[1,32,128]{2,1,0:T(8,128)(2,1)S(1)}, bf16[1,32,128]{2,1,0:T(8,128)(2,1)}, u32[]{:S(2)}) copy-start(bf16[1,32,128]{2,1,0:T(8,128)(2,1)} %param.4) | copy-start | bytes 24580
  2.8 19.5 %all-to-all-start.2 = ((bf16[8,136,128]{2,1,0:T(8,128)(2,1)}), bf16[8,136,128]{2,1,0:T(8,128)(2,1)S(1)}, u32[]{:S(2)}, u32[]{:S(2)}) async-start(bf16[8,136,128]{2,1,0:T(8,128)(2,1)} %broadcast_in_dim.44), calls=%async_computation.2 | async-start | bytes 557056 | tf_op jit(solution)/shard_map/all_to_all | solution.py:143
  56.4 12.2 %all-to-all-start.1 = ((bf16[4,16,40,128]{3,2,1,0:T(8,128)(2,1)}), bf16[4,16,40,128]{3,2,1,0:T(8,128)(2,1)S(1)}, u32[]{:S(2)}, u32[]{:S(2)}) async-start(bf16[4,16,40,128]{3,2,1,0:T(8,128)(2,1)} %broadcast_in_dim.41), calls=%async_computation.1 | async-start | bytes 1310720 | tf_op jit(solution)/shard_map/all_to_all | solution.py:143
  85.9 13.5 %all-to-all-start.3 = ((bf16[4,16,32,128]{3,2,1,0:T(8,128)(2,1)}), bf16[4,16,32,128]{3,2,1,0:T(8,128)(2,1)S(1)}, u32[]{:S(2)}, u32[]{:S(2)}) async-start(bf16[4,16,32,128]{3,2,1,0:T(8,128)(2,1)} %bitcast.5), calls=%async_computation.3 | async-start | bytes 1048576 | tf_op jit(solution)/shard_map/all_to_all | solution.py:147
  99.4 15.0 %all-to-all-start.6 = ((bf16[8,128,128]{2,1,0:T(8,128)(2,1)}), bf16[8,128,128]{2,1,0:T(8,128)(2,1)S(1)}, u32[]{:S(2)}, u32[]{:S(2)}) async-start(bf16[8,128,128]{2,1,0:T(8,128)(2,1)} %reduce_sum.44), calls=%async_computation.6 | async-start | bytes 524288 | tf_op jit(solution)/shard_map/all_to_all | solution.py:147
  114.3 17.2 %all-to-all-start.4 = ((bf16[16,32,128]{2,1,0:T(8,128)(2,1)}), bf16[16,32,128]{2,1,0:T(8,128)(2,1)S(1)}, u32[]{:S(2)}, u32[]{:S(2)}) async-start(bf16[16,32,128]{2,1,0:T(8,128)(2,1)} %reduce_sum.42), calls=%async_computation.4 | async-start | bytes 262144 | tf_op jit(solution)/shard_map/all_to_all | solution.py:147

commit v2 on v1

--- a/solution.py
+++ b/solution.py
@@ -14,7 +14,7 @@
 
 
 def pair_kernel(
-    caps_ref, vids_ref, dq_ref, dv_ref, own_dq_ref, own_dv_ref,
+    caps_ref, vids_ref, dq_ref, own_dq_ref, dv_kept_ref, dv_sent_ref,
     lift_ref, coef_ref, peak_ref, sum_ref, turned_ref, total_ref, mine_ref, *, q_len, v_len, lanes,
 ):
     cap_rows, vid_rows = caps_ref.shape[0], vids_ref.shape[0]
@@ -83,11 +83,13 @@
         dq_ref[pl.ds(block * block_caps, block_caps)] = turned.T.reshape(block_caps, q_len, features).astype(dq_ref.dtype)
         total_ref[...] += jnp.dot(coef, queries, preferred_element_type=jnp.float32)
 
-    dv_ref[...] = total_ref[...].reshape(dv_ref.shape).astype(dv_ref.dtype)
-
     own_scale = jnp.sum(mine_ref[...], axis=0, keepdims=True)
     coef = (lift_ref[own_block, own_vid] * own_scale).astype(jnp.bfloat16)
-    own_dv_ref[...] = jnp.dot(coef, queries_of(own_block), preferred_element_type=jnp.float32)
+    total_ref[pl.ds(own_vid * v_len, v_len), :] += jnp.dot(coef, queries_of(own_block), preferred_element_type=jnp.float32)
+    half = vid_rows // 2 * v_len
+    core = lax.axis_index("core")
+    dv_kept_ref[...] = total_ref[pl.ds(core * half, half), :].reshape(dv_kept_ref.shape)
+    dv_sent_ref[...] = total_ref[pl.ds((1 - core) * half, half), :].reshape(dv_sent_ref.shape).astype(dv_sent_ref.dtype)
     total_ref[pl.ds(0, lanes), :] = lax.dot_general(
         coef, vids_ref[own_vid, :v_len, :], (((0,), (0,)), ((), ())), preferred_element_type=jnp.float32
     )
@@ -101,9 +103,9 @@
         functools.partial(pair_kernel, q_len=q_len, v_len=v_len, lanes=lanes),
         out_shape=(
             jax.ShapeDtypeStruct((cap_rows, q_len, features), jnp.bfloat16),
-            jax.ShapeDtypeStruct((vid_rows, v_len, features), jnp.bfloat16),
             jax.ShapeDtypeStruct((q_len, features), jnp.float32),
-            jax.ShapeDtypeStruct((v_len, features), jnp.float32),
+            jax.ShapeDtypeStruct((vid_rows // 2, v_len, features), jnp.float32),
+            jax.ShapeDtypeStruct((vid_rows // 2, v_len, features), jnp.bfloat16),
         ),
         in_specs=[
             pl.BlockSpec(memory_space=pltpu.VMEM),
@@ -148,16 +150,32 @@
     return jnp.sum(moved.astype(jnp.float32), axis=0)
 
 
+def halve(kept, sent, axis, bit):
+    across = [(i, i ^ (1 << bit)) for i in range(lax.axis_size(axis))]
+    return kept + lax.ppermute(sent, axis, across).astype(jnp.float32)
+
+
+def sum_over_bits(kept, axis):
+    bits = lax.axis_size(axis).bit_length() - 1
+    for bit in range(bits):
+        kept = kept.reshape(-1, 2, *kept.shape[1:])
+        own = (lax.axis_index(axis) >> bit) & 1
+        sent = lax.dynamic_index_in_dim(kept, 1 - own, 1, keepdims=False)
+        kept = lax.dynamic_index_in_dim(kept, own, 1, keepdims=False)
+        kept = halve(kept, sent if bit == bits - 1 else sent.astype(jnp.bfloat16), axis, bit)
+    return kept[0]
+
+
 def local(caption_tokens, video_tokens, row_norms, col_norms):
     q_len, v_len, features = caption_tokens.shape[1], video_tokens.shape[1], caption_tokens.shape[2]
     x_count, y_count, z_count = lax.axis_size("x"), lax.axis_size("y"), lax.axis_size(Z)
     caps = spread_over(with_norm(caption_tokens, row_norms)[0], Z)
+    vids = lax.all_gather(with_norm(video_tokens, col_norms), "y", axis=0, tiled=True)
+    caps, vids = lax.optimization_barrier((caps, vids))
+    vids = lax.all_gather(vids, "core", axis=0, tiled=True)
     caps = spread_over(caps, "x").reshape(x_count * z_count, q_len + 8, features)
-    vids = spread_over(with_norm(video_tokens, col_norms)[0], "y")
-    vids = lax.all_gather(vids, "core", axis=0, tiled=True)
-    dq, dv, own_dq, own_dv = pair_grads(caps, vids, q_len, v_len)
-    dv = sum_over(dv.reshape(-1, y_count, v_len, features), "core").astype(jnp.bfloat16)
-    dv = (sum_over(dv, "y") + own_dv).astype(jnp.bfloat16)
+    dq, own_dq, dv_kept, dv_sent = pair_grads(caps, vids, q_len, v_len)
+    dv = sum_over_bits(halve(dv_kept, dv_sent, "core", 0), "y").astype(jnp.bfloat16)
     dq = sum_over(dq.reshape(x_count, z_count, q_len, features), "x").astype(jnp.bfloat16)
     dq = (sum_over(dq, Z) + own_dq).astype(jnp.bfloat16)
     return dq[None], dv[None]

time: 133 us -> 123 us (0.925)
  the two profiles are of different devices: /device:TPU:2 before, /device:TPU:8 now
where the time goes in v2:
time: 123 us; the launch traced here: 122 us
  starting transfers between devices  54.5 us (44%)
  blocking collectives  27.7 us (23%)
  waiting for transfers between devices  20.5 us (17%)
  Pallas kernels  13 us (11%)
  local copies, waits for them, and re-layouts  2.37 us (2%)
  other arithmetic  2.08 us (2%)
  between operations  2.08 us (2%)
    all_gather x1, blocking collectives, local(): lax.all_gather(with_norm(video_tokens, col_norms), 'y', axis=0, tiled=True)  25.5 us
    all_to_all x2, starting transfers between devices, spread_over(): return lax.all_to_all(copies, axis, 0, 0, tiled=True)  23.3 us
    ppermute x4, starting transfers between devices, halve(): return kept + lax.ppermute(sent, axis, across).astype(jnp.float32)  15.8 us
    all_to_all x2, starting transfers between devices, sum_over(): moved = lax.all_to_all(parts, axis, 0, 0, tiled=True)  15.3 us
    pallas_call x1, Pallas kernels, pair_grads(): pl.pallas_call(functools.partial(pair_kernel, q_len=q_len, v_len=v_len, l...  13 us
    all_to_all x2, waiting for transfers between devices, sum_over(): moved = lax.all_to_all(parts, axis, 0, 0, tiled=True)  8.01 us
    all_to_all x2, waiting for transfers between devices, spread_over(): return lax.all_to_all(copies, axis, 0, 0, tiled=True)  6.6 us
    ppermute x4, waiting for transfers between devices, halve(): return kept + lax.ppermute(sent, axis, across).astype(jnp.float32)  5.93 us
  transfers between devices with their start and end apart: 8, of which 6 were waited for; matrix products, arithmetic and copies ran while one was open for 1% of the time, Pallas kernels for 0%

profile of v2, /device:TPU:8, one launch (start us, length us, event | category | flops | bytes accessed | tf_op | source)
XLA Modules:
  0.0 122.3 jit_solution(7437260236770506997)
XLA Ops:
  1.3 0.7 pad_bitcast_fusion
  2.0 0.7 broadcast_in_dim.14
  2.7 0.0 copy-start
  2.7 19.0 %all-to-all-start = ((bf16[16,40,128]{2,1,0:T(8,128)(2,1)}), bf16[16,40,128]{2,1,0:T(8,128)(2,1)S(1)}, u32[]{:S(2)}, u32[]{:S(2)}) async-start(bf16[16,40,128]{2,1,0:T(8,128)(2,1)} %broadcast_in_dim.14), calls=%async_computation | async-start | bytes 327680 | tf_op jit(solution)/shard_map/all_to_all | solution.py:145
  22.3 0.0 copy-done
  22.3 25.5 %all_gather.6 = bf16[8,136,128]{2,1,0:T(8,128)(2,1)S(1)} all-gather(bf16[1,136,128]{2,1,0:T(8,128)(2,1)S(1)} %concatenate.7), channel_id=1, replica_groups=mesh['z_hi'=2,'y'=8,'x'=4,'z_lo'=8,'core'=2] {'y'}, dimensions={0}, use_global_device_ids=true | all-gather | bytes 313344 | tf_op jit(solution)/shard_map/all_gather | solution.py:173
  47.9 0.0 all-to-all-done
  47.9 0.9 broadcast_in_dim.16
  48.8 4.3 %all-to-all-start.1 = ((bf16[4,16,40,128]{3,2,1,0:T(8,128)(2,1)}), bf16[4,16,40,128]{3,2,1,0:T(8,128)(2,1)S(1)}, u32[]{:S(2)}, u32[]{:S(2)}) async-start(bf16[4,16,40,128]{3,2,1,0:T(8,128)(2,1)} %broadcast_in_dim.16), calls=%async_computation.1 | async-start | bytes 1310720 | tf_op jit(solution)/shard_map/all_to_all | solution.py:145
  53.1 2.2 %all_gather.7.vids_ref = bf16[16,136,128]{2,1,0:T(8,128)(2,1)S(1)} all-gather(bf16[8,136,128]{2,1,0:T(8,128)(2,1)S(1)} %all_gather.6), channel_id=1, replica_groups=mesh['z_hi'=2,'y'=8,'x'=4,'z_lo'=8,'core'=2] {'core'}, dimensions={0}, use_global_device_ids=true | all-gather | bytes 835584 | tf_op jit(solution)/shard_map/all_gather | solution.py:175
  55.3 6.6 %all-to-all-done.1 = bf16[4,16,40,128]{3,2,1,0:T(8,128)(2,1)S(1)} async-done(((bf16[4,16,40,128]{3,2,1,0:T(8,128)(2,1)}), bf16[4,16,40,128]{3,2,1,0:T(8,128)(2,1)S(1)}, u32[]{:S(2)}, u32[]{:S(2)}) %all-to-all-start.1) | async-done | bytes 655392 | tf_op jit(solution)/shard_map/all_to_all | solution.py:145
  61.9 13.0 %shard_map.59 = (bf16[64,32,128]{2,1,0:T(8,128)(2,1)}, f32[32,128]{1,0:T(8,128)S(1)}, f32[8,128,128]{2,1,0:T(8,128)S(1)}, bf16[8,128,128]{2,1,0:T(8,128)(2,1)S(1)}) custom-call(bf16[64,40,128]{2,1,0:T(8,128)(2,1)S(1)} %bitcast.24, bf16[16,136,128]{2,1,0:T(8,128)(2,1)S(1)} %all_gather.7.vids_ref), custom_call_target="tpu_custom_call" | custom-call | flops 3221225472 | bytes 2097152 | tf_op jit(solution)/shard_map/pallas_call | solution.py:102
  74.9 1.9 %collective-permute-start = (bf16[8,128,128]{2,1,0:T(8,128)(2,1)S(1)}, bf16[8,128,128]{2,1,0:T(8,128)(2,1)S(1)}, u32[]{:S(2)}, u32[]{:S(2)}) collective-permute-start(bf16[8,128,128]{2,1,0:T(8,128)(2,1)S(1)} %get-tuple-element.13), channel_id=1, source_target_pairs={{0,1},{1,0},{2,3},{3,2},{4,5},{5,4},{6,7},{7,6},{8,9},{9,8},{10,11... | collective-permute-start | bytes 786440 | tf_op jit(solution)/shard_map/ppermute | solution.py:155
  76.8 1.5 %collective-permute-done = bf16[8,128,128]{2,1,0:T(8,128)(2,1)S(1)} collective-permute-done((bf16[8,128,128]{2,1,0:T(8,128)(2,1)S(1)}, bf16[8,128,128]{2,1,0:T(8,128)(2,1)S(1)}, u32[]{:S(2)}, u32[]{:S(2)}) %collective-permute-start) | collective-permute-done | bytes 262176 | tf_op jit(solution)/shard_map/ppermute | solution.py:155
  78.4 3.4 %collective-permute-start.1 = (bf16[4,128,128]{2,1,0:T(8,128)(2,1)S(1)}, bf16[4,128,128]{2,1,0:T(8,128)(2,1)S(1)}, u32[]{:S(2)}, u32[]{:S(2)}) collective-permute-start(bf16[4,128,128]{2,1,0:T(8,128)(2,1)S(1)} %fusion), channel_id=1, source_target_pairs={{0,64},{64,0},{128,192},{192,128},{256,320},{320,256},{384,448},{4... | collective-permute-start | bytes 393224 | tf_op jit(solution)/shard_map/ppermute | solution.py:155
  81.9 3.5 %all-to-all-start.2 = ((bf16[4,16,32,128]{3,2,1,0:T(8,128)(2,1)}), bf16[4,16,32,128]{3,2,1,0:T(8,128)(2,1)S(1)}, u32[]{:S(2)}, u32[]{:S(2)}) async-start(bf16[4,16,32,128]{3,2,1,0:T(8,128)(2,1)} %bitcast.4), calls=%async_computation.2 | async-start | bytes 1048576 | tf_op jit(solution)/shard_map/all_to_all | solution.py:149
  85.3 0.5 collective-permute-done.1
  85.9 4.1 %collective-permute-start.2 = (bf16[2,128,128]{2,1,0:T(8,128)(2,1)S(1)}, bf16[2,128,128]{2,1,0:T(8,128)(2,1)S(1)}, u32[]{:S(2)}, u32[]{:S(2)}) collective-permute-start(bf16[2,128,128]{2,1,0:T(8,128)(2,1)S(1)} %fusion.1), channel_id=1, source_target_pairs={{0,128},{64,192},{128,0},{192,64},{256,384},{320,448},{384,256},{4... | collective-permute-start | bytes 196616 | tf_op jit(solution)/shard_map/ppermute | solution.py:155
  90.0 5.1 %all-to-all-done.2 = bf16[4,16,32,128]{3,2,1,0:T(8,128)(2,1)S(1)} async-done(((bf16[4,16,32,128]{3,2,1,0:T(8,128)(2,1)}), bf16[4,16,32,128]{3,2,1,0:T(8,128)(2,1)S(1)}, u32[]{:S(2)}, u32[]{:S(2)}) %all-to-all-start.2) | async-done | bytes 524320 | tf_op jit(solution)/shard_map/all_to_all | solution.py:149
  95.1 0.7 reduce_sum.21
  95.8 11.8 %all-to-all-start.3 = ((bf16[16,32,128]{2,1,0:T(8,128)(2,1)}), bf16[16,32,128]{2,1,0:T(8,128)(2,1)S(1)}, u32[]{:S(2)}, u32[]{:S(2)}) async-start(bf16[16,32,128]{2,1,0:T(8,128)(2,1)} %reduce_sum.21), calls=%async_computation.3 | async-start | bytes 262144 | tf_op jit(solution)/shard_map/all_to_all | solution.py:149
  107.7 0.0 collective-permute-done.2
  107.8 6.4 %collective-permute-start.3 = (f32[1,128,128]{2,1,0:T(8,128)S(1)}, f32[1,128,128]{2,1,0:T(8,128)S(1)}, u32[]{:S(2)}, u32[]{:S(2)}) collective-permute-start(f32[1,128,128]{2,1,0:T(8,128)S(1)} %constant_dynamic-slice_fusion), channel_id=1, source_target_pairs={{0,256},{64,320},{128,384},{192,448},{256,0},{320,64},{384,128},{4... | collective-permute-start | bytes 196616 | tf_op jit(solution)/shard_map/ppermute | solution.py:155
  114.1 3.9 %collective-permute-done.3 = f32[1,128,128]{2,1,0:T(8,128)S(1)} collective-permute-done((f32[1,128,128]{2,1,0:T(8,128)S(1)}, f32[1,128,128]{2,1,0:T(8,128)S(1)}, u32[]{:S(2)}, u32[]{:S(2)}) %collective-permute-start.3) | collective-permute-done | bytes 65568 | tf_op jit(solution)/shard_map/ppermute | solution.py:155
  118.1 0.6 add_convert_fusion
  118.7 2.9 %all-to-all-done.3 = bf16[16,32,128]{2,1,0:T(8,128)(2,1)S(1)} async-done(((bf16[16,32,128]{2,1,0:T(8,128)(2,1)}), bf16[16,32,128]{2,1,0:T(8,128)(2,1)S(1)}, u32[]{:S(2)}, u32[]{:S(2)}) %all-to-all-start.3) | async-done | bytes 131104 | tf_op jit(solution)/shard_map/all_to_all | solution.py:149
  121.7 0.6 fusion.2
  (8 shorter events, 0.2 us)
Async XLA Ops:
  2.7 19.7 %copy-start = (bf16[1,128,128]{2,1,0:T(8,128)(2,1)S(1)}, bf16[1,128,128]{2,1,0:T(8,128)(2,1)}, u32[]{:S(2)}) copy-start(bf16[1,128,128]{2,1,0:T(8,128)(2,1)} %param.5) | copy-start | bytes 98308
  2.7 45.2 %all-to-all-start = ((bf16[16,40,128]{2,1,0:T(8,128)(2,1)}), bf16[16,40,128]{2,1,0:T(8,128)(2,1)S(1)}, u32[]{:S(2)}, u32[]{:S(2)}) async-start(bf16[16,40,128]{2,1,0:T(8,128)(2,1)} %broadcast_in_dim.14), calls=%async_computation | async-start | bytes 327680 | tf_op jit(solution)/shard_map/all_to_all | solution.py:145
  48.8 13.1 %all-to-all-start.1 = ((bf16[4,16,40,128]{3,2,1,0:T(8,128)(2,1)}), bf16[4,16,40,128]{3,2,1,0:T(8,128)(2,1)S(1)}, u32[]{:S(2)}, u32[]{:S(2)}) async-start(bf16[4,16,40,128]{3,2,1,0:T(8,128)(2,1)} %broadcast_in_dim.16), calls=%async_computation.1 | async-start | bytes 1310720 | tf_op jit(solution)/shard_map/all_to_all | solution.py:145
  74.9 3.4 %collective-permute-start = (bf16[8,128,128]{2,1,0:T(8,128)(2,1)S(1)}, bf16[8,128,128]{2,1,0:T(8,128)(2,1)S(1)}, u32[]{:S(2)}, u32[]{:S(2)}) collective-permute-start(bf16[8,128,128]{2,1,0:T(8,128)(2,1)S(1)} %get-tuple-element.13), channel_id=1, source_target_pairs={{0,1},{1,0},{2,3},{3,2},{4,5},{5,4},{6,7},{7,6},{8,9},{9,8},{10,11... | collective-permute-start | bytes 786440 | tf_op jit(solution)/shard_map/ppermute | solution.py:155
  78.4 7.4 %collective-permute-start.1 = (bf16[4,128,128]{2,1,0:T(8,128)(2,1)S(1)}, bf16[4,128,128]{2,1,0:T(8,128)(2,1)S(1)}, u32[]{:S(2)}, u32[]{:S(2)}) collective-permute-start(bf16[4,128,128]{2,1,0:T(8,128)(2,1)S(1)} %fusion), channel_id=1, source_target_pairs={{0,64},{64,0},{128,192},{192,128},{256,320},{320,256},{384,448},{4... | collective-permute-start | bytes 393224 | tf_op jit(solution)/shard_map/ppermute | solution.py:155
  81.9 13.2 %all-to-all-start.2 = ((bf16[4,16,32,128]{3,2,1,0:T(8,128)(2,1)}), bf16[4,16,32,128]{3,2,1,0:T(8,128)(2,1)S(1)}, u32[]{:S(2)}, u32[]{:S(2)}) async-start(bf16[4,16,32,128]{3,2,1,0:T(8,128)(2,1)} %bitcast.4), calls=%async_computation.2 | async-start | bytes 1048576 | tf_op jit(solution)/shard_map/all_to_all | solution.py:149
  85.9 21.8 %collective-permute-start.2 = (bf16[2,128,128]{2,1,0:T(8,128)(2,1)S(1)}, bf16[2,128,128]{2,1,0:T(8,128)(2,1)S(1)}, u32[]{:S(2)}, u32[]{:S(2)}) collective-permute-start(bf16[2,128,128]{2,1,0:T(8,128)(2,1)S(1)} %fusion.1), channel_id=1, source_target_pairs={{0,128},{64,192},{128,0},{192,64},{256,384},{320,448},{384,256},{4... | collective-permute-start | bytes 196616 | tf_op jit(solution)/shard_map/ppermute | solution.py:155
  95.8 25.8 %all-to-all-start.3 = ((bf16[16,32,128]{2,1,0:T(8,128)(2,1)}), bf16[16,32,128]{2,1,0:T(8,128)(2,1)S(1)}, u32[]{:S(2)}, u32[]{:S(2)}) async-start(bf16[16,32,128]{2,1,0:T(8,128)(2,1)} %reduce_sum.21), calls=%async_computation.3 | async-start | bytes 262144 | tf_op jit(solution)/shard_map/all_to_all | solution.py:149
  107.8 10.3 %collective-permute-start.3 = (f32[1,128,128]{2,1,0:T(8,128)S(1)}, f32[1,128,128]{2,1,0:T(8,128)S(1)}, u32[]{:S(2)}, u32[]{:S(2)}) collective-permute-start(f32[1,128,128]{2,1,0:T(8,128)S(1)} %constant_dynamic-slice_fusion), channel_id=1, source_target_pairs={{0,256},{64,320},{128,384},{192,448},{256,0},{320,64},{384,128},{4... | collective-permute-start | bytes 196616 | tf_op jit(solution)/shard_map/ppermute | solution.py:155

commit v3 on v2

--- a/solution.py
+++ b/solution.py
@@ -150,32 +150,18 @@
     return jnp.sum(moved.astype(jnp.float32), axis=0)
 
 
-def halve(kept, sent, axis, bit):
-    across = [(i, i ^ (1 << bit)) for i in range(lax.axis_size(axis))]
-    return kept + lax.ppermute(sent, axis, across).astype(jnp.float32)
-
-
-def sum_over_bits(kept, axis):
-    bits = lax.axis_size(axis).bit_length() - 1
-    for bit in range(bits):
-        kept = kept.reshape(-1, 2, *kept.shape[1:])
-        own = (lax.axis_index(axis) >> bit) & 1
-        sent = lax.dynamic_index_in_dim(kept, 1 - own, 1, keepdims=False)
-        kept = lax.dynamic_index_in_dim(kept, own, 1, keepdims=False)
-        kept = halve(kept, sent if bit == bits - 1 else sent.astype(jnp.bfloat16), axis, bit)
-    return kept[0]
-
-
 def local(caption_tokens, video_tokens, row_norms, col_norms):
     q_len, v_len, features = caption_tokens.shape[1], video_tokens.shape[1], caption_tokens.shape[2]
-    x_count, y_count, z_count = lax.axis_size("x"), lax.axis_size("y"), lax.axis_size(Z)
+    x_count, z_count = lax.axis_size("x"), lax.axis_size(Z)
     caps = spread_over(with_norm(caption_tokens, row_norms)[0], Z)
-    vids = lax.all_gather(with_norm(video_tokens, col_norms), "y", axis=0, tiled=True)
+    vids = with_norm(video_tokens, col_norms)
     caps, vids = lax.optimization_barrier((caps, vids))
+    vids = spread_over(vids[0], "y")
+    caps = lax.all_gather(caps, "x", axis=0, tiled=True)
     vids = lax.all_gather(vids, "core", axis=0, tiled=True)
-    caps = spread_over(caps, "x").reshape(x_count * z_count, q_len + 8, features)
     dq, own_dq, dv_kept, dv_sent = pair_grads(caps, vids, q_len, v_len)
-    dv = sum_over_bits(halve(dv_kept, dv_sent, "core", 0), "y").astype(jnp.bfloat16)
+    dv = dv_kept + lax.ppermute(dv_sent, "core", [(0, 1), (1, 0)]).astype(jnp.float32)
+    dv = lax.psum_scatter(dv, "y", scatter_dimension=0, tiled=False).astype(jnp.bfloat16)
     dq = sum_over(dq.reshape(x_count, z_count, q_len, features), "x").astype(jnp.bfloat16)
     dq = (sum_over(dq, Z) + own_dq).astype(jnp.bfloat16)
     return dq[None], dv[None]

time: 123 us -> 139 us (1.13)
  starting transfers between devices: 54.5 us -> 32.3 us
  waiting for transfers between devices: 20.5 us -> 37.8 us
  between operations: 2.08 us -> 15.4 us
  blocking collectives: 27.7 us -> 34.7 us
    all_to_all x0 -> x1, blocking collectives: none -> 18.6 us  [sum_over(): moved = lax.all_to_all(parts, axis, 0, 0, tiled=True)]
    ppermute x4 -> x1, starting transfers between devices: 15.8 us -> 2.04 us  [local(): lax.ppermute(dv_sent, 'core', [(0, 1), (1, 0)]).astype(jnp.float32)]
    reduce_scatter x0 -> x1, waiting for transfers between devices: none -> 13.7 us  [local(): lax.psum_scatter(dv, 'y', scatter_dimension=0, tiled=False)]
    all_gather x1, blocking collectives: 25.5 us -> 13.9 us  [local(): caps = lax.all_gather(caps, 'x', axis=0, tiled=True)]
    all_to_all x2 -> x1, starting transfers between devices: 15.3 us -> 3.71 us  [sum_over(): moved = lax.all_to_all(parts, axis, 0, 0, tiled=True)]
    all_to_all x2, waiting for transfers between devices: 6.6 us -> 15 us  [spread_over(): return lax.all_to_all(copies, axis, 0, 0, tiled=True)]
    ppermute x4 -> x1, waiting for transfers between devices: 5.93 us -> 0.01 us  [local(): lax.ppermute(dv_sent, 'core', [(0, 1), (1, 0)]).astype(jnp.float32)]
    all_to_all x2, starting transfers between devices: 23.3 us -> 26.5 us  [spread_over(): return lax.all_to_all(copies, axis, 0, 0, tiled=True)]
  transfers between devices with their start and end apart: 8 -> 5, of which waited for: 6 -> 3; matrix products, arithmetic and copies ran while one was open for 1% -> 1% of each run, Pallas kernels for 0% -> 0%
where the time goes in v3:
time: 139 us; the launch traced here: 138 us
  waiting for transfers between devices  37.8 us (27%)
  blocking collectives  34.7 us (25%)
  starting transfers between devices  32.3 us (23%)
  between operations  15.4 us (11%)
  Pallas kernels  13 us (9%)
  other arithmetic  3 us (2%)
  local copies, waits for them, and re-layouts  2.12 us (2%)
    all_to_all x2, starting transfers between devices, spread_over(): return lax.all_to_all(copies, axis, 0, 0, tiled=True)  26.5 us
    all_to_all x1, blocking collectives, sum_over(): moved = lax.all_to_all(parts, axis, 0, 0, tiled=True)  18.6 us
    all_to_all x2, waiting for transfers between devices, spread_over(): return lax.all_to_all(copies, axis, 0, 0, tiled=True)  15 us
    all_gather x1, blocking collectives, local(): caps = lax.all_gather(caps, 'x', axis=0, tiled=True)  13.9 us
    reduce_scatter x1, waiting for transfers between devices, local(): lax.psum_scatter(dv, 'y', scatter_dimension=0, tiled=False)  13.7 us
    pallas_call x1, Pallas kernels, pair_grads(): pl.pallas_call(functools.partial(pair_kernel, q_len=q_len, v_len=v_len, l...  13 us
    all_to_all x1, waiting for transfers between devices, sum_over(): moved = lax.all_to_all(parts, axis, 0, 0, tiled=True)  9.16 us
    all_to_all x1, starting transfers between devices, sum_over(): moved = lax.all_to_all(parts, axis, 0, 0, tiled=True)  3.71 us
  transfers between devices with their start and end apart: 5, of which 3 were waited for; matrix products, arithmetic and copies ran while one was open for 1% of the time, Pallas kernels for 0%

profile of v3, /device:TPU:8, one launch (start us, length us, event | category | flops | bytes accessed | tf_op | source)
XLA Modules:
  0.0 138.3 jit_solution(3629905769394680250)
XLA Ops:
  7.8 0.7 pad_bitcast_fusion
  8.5 0.7 broadcast_in_dim.32
  9.2 0.0 copy-start
  9.2 19.0 %all-to-all-start = ((bf16[16,40,128]{2,1,0:T(8,128)(2,1)}), bf16[16,40,128]{2,1,0:T(8,128)(2,1)S(1)}, u32[]{:S(2)}, u32[]{:S(2)}) async-start(bf16[16,40,128]{2,1,0:T(8,128)(2,1)} %broadcast_in_dim.32), calls=%async_computation | async-start | bytes 327680 | tf_op jit(solution)/shard_map/all_to_all | solution.py:145
  28.9 0.0 copy-done
  28.9 15.0 %all-to-all-done = bf16[16,40,128]{2,1,0:T(8,128)(2,1)S(1)} async-done(((bf16[16,40,128]{2,1,0:T(8,128)(2,1)}), bf16[16,40,128]{2,1,0:T(8,128)(2,1)S(1)}, u32[]{:S(2)}, u32[]{:S(2)}) %all-to-all-start) | async-done | bytes 163872 | tf_op jit(solution)/shard_map/all_to_all | solution.py:145
  43.8 0.7 broadcast_in_dim.35
  44.6 7.5 %all-to-all-start.1 = ((bf16[8,136,128]{2,1,0:T(8,128)(2,1)}), bf16[8,136,128]{2,1,0:T(8,128)(2,1)S(1)}, u32[]{:S(2)}, u32[]{:S(2)}) async-start(bf16[8,136,128]{2,1,0:T(8,128)(2,1)} %broadcast_in_dim.35), calls=%async_computation.1 | async-start | bytes 557056 | tf_op jit(solution)/shard_map/all_to_all | solution.py:145
  52.1 13.9 %all_gather.6.caps_ref = bf16[64,40,128]{2,1,0:T(8,128)(2,1)S(1)} all-gather(bf16[16,40,128]{2,1,0:T(8,128)(2,1)S(1)} %all-to-all-done), channel_id=1, replica_groups=mesh['z_hi'=2,'y'=8,'x'=4,'z_lo'=8,'core'=2] {'x'}, dimensions={0}, use_global_device_ids=true | all-gather | bytes 819200 | tf_op jit(solution)/shard_map/all_gather | solution.py:160
  66.0 0.0 all-to-all-done.1
  66.0 2.2 %all_gather.7.vids_ref = bf16[16,136,128]{2,1,0:T(8,128)(2,1)S(1)} all-gather(bf16[8,136,128]{2,1,0:T(8,128)(2,1)S(1)} %all-to-all-done.1), channel_id=1, replica_groups=mesh['z_hi'=2,'y'=8,'x'=4,'z_lo'=8,'core'=2] {'core'}, dimensions={0}, use_global_device_ids=true | all-gather | bytes 835584 | tf_op jit(solution)/shard_map/all_gather | solution.py:161
  68.2 13.0 %shard_map.59 = (bf16[64,32,128]{2,1,0:T(8,128)(2,1)}, f32[32,128]{1,0:T(8,128)S(1)}, f32[8,128,128]{2,1,0:T(8,128)S(1)}, bf16[8,128,128]{2,1,0:T(8,128)(2,1)S(1)}) custom-call(bf16[64,40,128]{2,1,0:T(8,128)(2,1)S(1)} %all_gather.6.caps_ref, bf16[16,136,128]{2,1,0:T(8,128)(2,1)S(1)} %all_gather.7.vids_ref), custom_call_target="tpu_custom_call" | custom-call | flops 3221225472 | bytes 2097152 | tf_op jit(solution)/shard_map/pallas_call | solution.py:102
  81.2 2.0 %collective-permute-start = (bf16[8,128,128]{2,1,0:T(8,128)(2,1)S(1)}, bf16[8,128,128]{2,1,0:T(8,128)(2,1)S(1)}, u32[]{:S(2)}, u32[]{:S(2)}) collective-permute-start(bf16[8,128,128]{2,1,0:T(8,128)(2,1)S(1)} %get-tuple-element.13), channel_id=1, source_target_pairs={{0,1},{1,0},{2,3},{3,2},{4,5},{5,4},{6,7},{7,6},{8,9},{9,8},{10,11... | collective-permute-start | bytes 786440 | tf_op jit(solution)/shard_map/ppermute | solution.py:163
  83.2 3.7 %all-to-all-start.2 = ((bf16[4,16,32,128]{3,2,1,0:T(8,128)(2,1)}), bf16[4,16,32,128]{3,2,1,0:T(8,128)(2,1)S(1)}, u32[]{:S(2)}, u32[]{:S(2)}) async-start(bf16[4,16,32,128]{3,2,1,0:T(8,128)(2,1)} %bitcast.4), calls=%async_computation.2 | async-start | bytes 1048576 | tf_op jit(solution)/shard_map/all_to_all | solution.py:149
  87.0 0.0 reduce-scatter.2.cloned.1.call-start
  87.0 0.0 collective-permute-done
  87.0 0.8 convert_add_fusion
  87.8 0.0 reduce-scatter.2.cloned.1.call-update
  87.8 9.2 %all-to-all-done.2 = bf16[4,16,32,128]{3,2,1,0:T(8,128)(2,1)S(1)} async-done(((bf16[4,16,32,128]{3,2,1,0:T(8,128)(2,1)}), bf16[4,16,32,128]{3,2,1,0:T(8,128)(2,1)S(1)}, u32[]{:S(2)}, u32[]{:S(2)}) %all-to-all-start.2) | async-done | bytes 524320 | tf_op jit(solution)/shard_map/all_to_all | solution.py:149
  97.0 0.1 reduce_sum.21
  97.1 18.6 %all_to_all.20 = bf16[16,32,128]{2,1,0:T(8,128)(2,1)S(1)} all-to-all(bf16[16,32,128]{2,1,0:T(8,128)(2,1)S(1)} %reduce_sum.21), channel_id=1, replica_groups=mesh['z_hi'=2,'y'=8,'x'=4,'z_lo'=8,'core'=2] {'z_hi','z_lo'}, dimensions={0} | all-to-all | bytes 262144 | tf_op jit(solution)/shard_map/all_to_all | solution.py:149
  115.7 0.6 fusion
  116.3 13.7 %reduce-scatter.2.cloned.1.call-done = f32[1,128,128]{2,1,0:T(8,128)} async-done(((f32[8,128,128]{2,1,0:T(8,128)}), f32[1,128,128]{2,1,0:T(8,128)}) %reduce-scatter.2.cloned.1.call-update) | async-done | bytes 65552 | tf_op jit(solution)/shard_map/reduce_scatter | solution.py:164
  130.0 1.5 %convert_element_type.18 = bf16[1,128,128]{2,1,0:T(8,128)(2,1)} convert(f32[1,128,128]{2,1,0:T(8,128)} %reduce-scatter.2.cloned.1.call-done) | non-fusion elementwise | flops 16384 | bytes 98304 | tf_op jit(solution)/shard_map/convert_element_type | solution.py:164
  (2 shorter events, 0.0 us)
Async XLA Ops:
  9.2 19.7 %copy-start = (bf16[1,128,128]{2,1,0:T(8,128)(2,1)S(1)}, bf16[1,128,128]{2,1,0:T(8,128)(2,1)}, u32[]{:S(2)}) copy-start(bf16[1,128,128]{2,1,0:T(8,128)(2,1)} %param.5) | copy-start | bytes 98308
  9.2 34.6 %all-to-all-start = ((bf16[16,40,128]{2,1,0:T(8,128)(2,1)}), bf16[16,40,128]{2,1,0:T(8,128)(2,1)S(1)}, u32[]{:S(2)}, u32[]{:S(2)}) async-start(bf16[16,40,128]{2,1,0:T(8,128)(2,1)} %broadcast_in_dim.32), calls=%async_computation | async-start | bytes 327680 | tf_op jit(solution)/shard_map/all_to_all | solution.py:145
  44.6 21.4 %all-to-all-start.1 = ((bf16[8,136,128]{2,1,0:T(8,128)(2,1)}), bf16[8,136,128]{2,1,0:T(8,128)(2,1)S(1)}, u32[]{:S(2)}, u32[]{:S(2)}) async-start(bf16[8,136,128]{2,1,0:T(8,128)(2,1)} %broadcast_in_dim.35), calls=%async_computation.1 | async-start | bytes 557056 | tf_op jit(solution)/shard_map/all_to_all | solution.py:145
  81.2 5.8 %collective-permute-start = (bf16[8,128,128]{2,1,0:T(8,128)(2,1)S(1)}, bf16[8,128,128]{2,1,0:T(8,128)(2,1)S(1)}, u32[]{:S(2)}, u32[]{:S(2)}) collective-permute-start(bf16[8,128,128]{2,1,0:T(8,128)(2,1)S(1)} %get-tuple-element.13), channel_id=1, source_target_pairs={{0,1},{1,0},{2,3},{3,2},{4,5},{5,4},{6,7},{7,6},{8,9},{9,8},{10,11... | collective-permute-start | bytes 786440 | tf_op jit(solution)/shard_map/ppermute | solution.py:163
  83.2 13.7 %all-to-all-start.2 = ((bf16[4,16,32,128]{3,2,1,0:T(8,128)(2,1)}), bf16[4,16,32,128]{3,2,1,0:T(8,128)(2,1)S(1)}, u32[]{:S(2)}, u32[]{:S(2)}) async-start(bf16[4,16,32,128]{3,2,1,0:T(8,128)(2,1)} %bitcast.4), calls=%async_computation.2 | async-start | bytes 1048576 | tf_op jit(solution)/shard_map/all_to_all | solution.py:149
  87.0 43.0 %reduce-scatter.2.cloned.1.call-start = ((), (), s32[]{:S(2)}) async-start(), calls=%async_computation.5 | async-start | bytes 589824 | tf_op jit(solution)/shard_map/reduce_scatter | solution.py:164
Sparse Core Ops, SparseCore 0:
  91.2 38.7 reduce-scatter.1

commit v4 on v3

v4 whole, which is shorter than its diff:
```python
import functools
import math

import jax
import jax.numpy as jnp
from jax import lax
from jax.experimental import pallas as pl
from jax.experimental.pallas import tpu as pltpu
from jax.sharding import Mesh
from jax.sharding import PartitionSpec as P

pool_tau = 0.05
logit_temp = 0.5


def block_queries(caps_ref, block, lanes, q_len):
    block_caps = lanes // q_len
    return caps_ref[pl.ds(block * block_caps, block_caps), :q_len, :].reshape(lanes, caps_ref.shape[2])


def video_kernel(
    caps_ref, vids_ref, kept_ref, sent_ref, turned_ref, out_ref,
    lift_ref, peak_ref, sum_ref, total_ref, coef_ref, done, *, q_len, v_len, lanes,
):
    cap_rows, vid_rows = caps_ref.shape[0], vids_ref.shape[0]
    features = caps_ref.shape[2]
    block_caps = lanes // q_len
    blocks = cap_rows // block_caps
    to_exp2 = 1.0 / (pool_tau * math.log(2.0))

    own_cap = lax.axis_index("x") * lax.axis_size(Z) + lax.axis_index("z_hi") * lax.axis_size("z_lo") + lax.axis_index("z_lo")
    own_vid = lax.axis_index("core") * lax.axis_size("y") + lax.axis_index("y")

    turned_ref[...] = vids_ref[:, :v_len, :].reshape(vid_rows * v_len, features).T
    total_ref[...] = jnp.zeros_like(total_ref)

    @pl.loop(0, blocks)
    def _(block):
        queries = block_queries(caps_ref, block, lanes, q_len)
        for v in range(vid_rows):
            scores = lax.dot_general(
                vids_ref[v, :v_len, :], queries, (((1,), (1,)), ((), ())), preferred_element_type=jnp.float32
            )
            peak = jnp.max(scores, axis=0, keepdims=True)
            lifted = jnp.exp2((scores - peak) * to_exp2)
            lift_ref[block, v] = lifted
            peak_ref[block, pl.ds(v, 1), :] = peak
            sum_ref[block, pl.ds(v, 1), :] = jnp.sum(lifted, axis=0, keepdims=True)

    q_bits = q_len.bit_length() - 1
    row = lax.broadcasted_iota(jnp.int32, (lanes, lanes), 0) >> q_bits
    col = lax.broadcasted_iota(jnp.int32, (lanes, lanes), 1) >> q_bits
    spread = jnp.where(row == col, 1.0 / (q_len * logit_temp), 0.0)
    col_norm = vids_ref[:, v_len, :1].astype(jnp.float32)
    lane_cap = lax.broadcasted_iota(jnp.int32, (vid_rows, lanes), 1) >> q_bits
    sub_vid = lax.broadcasted_iota(jnp.int32, (vid_rows, lanes), 0)

    for block in range(blocks):
        summed = sum_ref[block]
        pooled = peak_ref[block] + pool_tau * jnp.log(summed)
        logits = jnp.dot(pooled, spread, preferred_element_type=jnp.float32, precision=lax.Precision.HIGHEST)
        row_norm = jnp.zeros((1, lanes), jnp.float32)
        for c in range(block_caps):
            norm = caps_ref[block * block_caps + c, pl.ds(q_len, 1), :].astype(jnp.float32)
            norm = jnp.concatenate([norm] * (lanes // norm.shape[1]), axis=1)
            row_norm = jnp.where(lane_cap[:1] == c, norm, row_norm)
        paired = (lane_cap + block * block_caps == own_cap) & (sub_vid == own_vid)
        pair_grad = (jnp.exp(logits - row_norm) + jnp.exp(logits - col_norm) - 2.0 * paired.astype(jnp.float32)) / (2.0 * logit_temp)
        sum_ref[block] = pair_grad / (summed * q_len)

    @pl.loop(0, blocks)
    def _(block):
        for v in range(vid_rows):
            coef_ref[block, pl.ds(v * v_len, v_len), :] = (lift_ref[block, v] * sum_ref[block, pl.ds(v, 1), :]).astype(jnp.bfloat16)
        pltpu.make_async_copy(coef_ref.at[block], out_ref.at[block], done.at[block]).start()
        total_ref[...] += jnp.dot(coef_ref[block], block_queries(caps_ref, block, lanes, q_len), preferred_element_type=jnp.float32)

    half = vid_rows // 2 * v_len
    core = lax.axis_index("core")
    kept_ref[...] = total_ref[pl.ds(core * half, half), :].reshape(kept_ref.shape)
    sent_ref[...] = total_ref[pl.ds((1 - core) * half, half), :].reshape(sent_ref.shape).astype(sent_ref.dtype)
    for block in range(blocks):
        pltpu.make_async_copy(coef_ref.at[block], out_ref.at[block], done.at[block]).wait()


def caption_kernel(in_ref, turned_ref, *refs):
    *sum_refs, coef_ref, done = refs
    x_count = len(sum_refs)
    x_blocks = coef_ref.shape[0] // x_count
    lanes, features = coef_ref.shape[2], turned_ref.shape[0]
    q_len = sum_refs[0].shape[1]
    block_caps = lanes // q_len

    def copy(away, part):
        place, slot = lax.rem(lax.axis_index("x") + away, x_count), away * x_blocks + part
        return pltpu.make_async_copy(in_ref.at[place * x_blocks + part], coef_ref.at[slot], done.at[slot])

    for away in range(x_count):
        for part in range(x_blocks):
            copy(away, part).start()
    for away, ref in enumerate(sum_refs):
        for part in range(x_blocks):
            copy(away, part).wait()
            turned = jnp.dot(turned_ref[...], coef_ref[away * x_blocks + part], preferred_element_type=jnp.float32)
            ref[pl.ds(part * block_caps, block_caps)] = turned.T.reshape(block_caps, q_len, features).astype(ref.dtype)


def video_grads(caps, vids, q_len, v_len, lanes=256):
    cap_rows, vid_rows, features = caps.shape[0], vids.shape[0], caps.shape[2]
    blocks = cap_rows * q_len // lanes
    pairs = cap_rows * q_len * vid_rows * v_len
    return pl.pallas_call(
        functools.partial(video_kernel, q_len=q_len, v_len=v_len, lanes=lanes),
        out_shape=(
            jax.ShapeDtypeStruct((vid_rows // 2, v_len, features), jnp.float32),
            jax.ShapeDtypeStruct((vid_rows // 2, v_len, features), jnp.bfloat16),
            jax.ShapeDtypeStruct((features, vid_rows * v_len), jnp.bfloat16),
            jax.ShapeDtypeStruct((blocks, vid_rows * v_len, lanes), jnp.bfloat16),
        ),
        in_specs=[pl.BlockSpec(memory_space=pltpu.VMEM)] * 2,
        out_specs=[pl.BlockSpec(memory_space=pltpu.VMEM)] * 3 + [pl.BlockSpec(memory_space=pl.ANY)],
        scratch_shapes=[
            pltpu.VMEM((blocks, vid_rows, v_len, lanes), jnp.float32),
            pltpu.VMEM((blocks, vid_rows, lanes), jnp.float32),
            pltpu.VMEM((blocks, vid_rows, lanes), jnp.float32),
            pltpu.VMEM((vid_rows * v_len, features), jnp.float32),
            pltpu.VMEM((blocks, vid_rows * v_len, lanes), jnp.bfloat16),
            pltpu.SemaphoreType.DMA((blocks,)),
        ],
        compiler_params=pltpu.CompilerParams(vmem_limit_bytes=51 * 2**20),
        cost_estimate=pl.CostEstimate(flops=4 * pairs * features, bytes_accessed=2 * pairs, transcendentals=pairs),
    )(caps, vids)


def caption_grads(coef, turned, x_count, z_count, q_len):
    features = turned.shape[0]
    return pl.pallas_call(
        caption_kernel,
        out_shape=tuple(
            jax.ShapeDtypeStruct((z_count, q_len, features), jnp.bfloat16 if away else jnp.float32) for away in range(x_count)
        ),
        in_specs=[pl.BlockSpec(memory_space=pl.ANY), pl.BlockSpec(memory_space=pltpu.VMEM)],
        out_specs=[pl.BlockSpec(memory_space=pltpu.VMEM)] * x_count,
        scratch_shapes=[pltpu.VMEM(coef.shape, coef.dtype), pltpu.SemaphoreType.DMA((coef.shape[0],))],
        compiler_params=pltpu.CompilerParams(vmem_limit_bytes=51 * 2**20),
        cost_estimate=pl.CostEstimate(flops=2 * coef.size * features, bytes_accessed=2 * coef.size, transcendentals=0),
    )(coef, turned)


PARTS = (2, 8, 4, 8, 2)
AXES = ("z_hi", "y", "x", "z_lo", "core")
Z = ("z_hi", "z_lo")


def with_norm(tokens, norm):
    return jnp.concatenate([tokens, jnp.broadcast_to(norm[:, None, None], (1, 8, tokens.shape[2]))], axis=1)


def spread_over(block, axis):
    size = lax.axis_size(axis)
    copies = jnp.broadcast_to(block[None], (size, *block.shape))
    return lax.all_to_all(copies, axis, 0, 0, tiled=True)


def send(sums, axis):
    return lax.all_to_all(sums.astype(jnp.bfloat16), axis, 0, 0, tiled=True)


def add_up(sums, moved, axis):
    place = lax.axis_index(axis)
    others = lax.broadcasted_iota(jnp.int32, sums.shape, 0) != place
    own = lax.dynamic_index_in_dim(sums, place, 0, keepdims=False)
    return (jnp.sum(jnp.where(others, moved.astype(jnp.float32), 0.0), axis=0) + own).astype(jnp.bfloat16)


def local(caption_tokens, video_tokens, row_norms, col_norms):
    q_len, v_len, features = caption_tokens.shape[1], video_tokens.shape[1], caption_tokens.shape[2]
    x_count, z_count = lax.axis_size("x"), lax.axis_size(Z)
    caps = spread_over(with_norm(caption_tokens, row_norms)[0], Z)
    vids = with_norm(video_tokens, col_norms)
    caps, vids = lax.optimization_barrier((caps, vids))
    vids = spread_over(vids[0], "y")
    caps = lax.all_gather(caps, "x", axis=0, tiled=True)
    vids = lax.all_gather(vids, "core", axis=0, tiled=True)
    dv, dv_sent, turned, coef = video_grads(caps, vids, q_len, v_len)
    dv = dv + lax.ppermute(dv_sent, "core", [(0, 1), (1, 0)]).astype(jnp.float32)
    dv, turned = lax.optimization_barrier((dv, turned))
    dv_moved = send(dv, "y")
    dq, *dq_sent = caption_grads(coef, turned, x_count, z_count, q_len)
    for away, sent in enumerate(dq_sent, 1):
        dq = dq + lax.ppermute(sent, "x", [(i, (i + away) % x_count) for i in range(x_count)]).astype(jnp.float32)
    dq, dv_moved = lax.optimization_barrier((dq, dv_moved))
    return add_up(dq, send(dq, Z), Z)[None], add_up(dv, dv_moved, "y")[None]


def solution(mesh):
    fine = Mesh(mesh.devices.reshape(PARTS), AXES)
    return jax.shard_map(
        local,
        mesh=fine,
        in_specs=(P(AXES, None, None), P(AXES, None, None), P(AXES), P(AXES)),
        out_specs=(P(AXES, None, None), P(AXES, None, None)),
        check_vma=False,
    )
```

time: 139 us -> 124 us (0.89)
  blocking collectives: 34.7 us -> 16.1 us
  starting transfers between devices: 32.3 us -> 49.9 us
  between operations: 15.4 us -> 2.07 us
  waiting for transfers between devices: 37.8 us -> 33 us
  Pallas kernels: 13 us -> 16.4 us
    all_to_all x1 -> x0, blocking collectives: 18.6 us -> none  [sum_over(): moved = lax.all_to_all(parts, axis, 0, 0, tiled=True)]
    reduce_scatter x1 -> x0, waiting for transfers between devices: 13.7 us -> none  [local(): lax.psum_scatter(dv, 'y', scatter_dimension=0, tiled=False)]
    ppermute x0 -> x3, starting transfers between devices: none -> 9.9 us  [local(): lax.ppermute(sent, 'x', [(i, (i + away) % x_count) for i in range(x_count)])]
    all_to_all x1 -> x2, starting transfers between devices: 3.71 us -> 11.5 us  [send(): return lax.all_to_all(sums.astype(jnp.bfloat16), axis, 0, 0, tiled=True)]
    ppermute x0 -> x3, waiting for transfers between devices: none -> 4.92 us  [local(): lax.ppermute(sent, 'x', [(i, (i + away) % x_count) for i in range(x_count)])]
    pallas_call x1 -> x2, Pallas kernels: 13 us -> 16.4 us  [the longest x1 11.2 us: video_grads(): pl.pallas_call(functools.partial(video_kernel, q_len=q_len, v_len=v_len,...]
    all_to_all x1 -> x2, waiting for transfers between devices: 9.16 us -> 12.5 us  [send(): return lax.all_to_all(sums.astype(jnp.bfloat16), axis, 0, 0, tiled=True)]
  transfers between devices with their start and end apart: 5 -> 8, of which waited for: 3 -> 5; matrix products, arithmetic and copies ran while one was open for 1% -> 1% of each run, Pallas kernels for 0% -> 4%
where the time goes in v4:
time: 124 us; the launch traced here: 123 us
  starting transfers between devices  49.9 us (40%)
  waiting for transfers between devices  33 us (27%)
  Pallas kernels  16.4 us (13%)
  blocking collectives  16.1 us (13%)
  other arithmetic  3 us (2%)
  local copies, waits for them, and re-layouts  2.88 us (2%)
  between operations  2.07 us (2%)
    all_to_all x2, starting transfers between devices, spread_over(): return lax.all_to_all(copies, axis, 0, 0, tiled=True)  26.4 us
    all_to_all x2, waiting for transfers between devices, spread_over(): return lax.all_to_all(copies, axis, 0, 0, tiled=True)  14.2 us
    all_gather x1, blocking collectives, local(): caps = lax.all_gather(caps, 'x', axis=0, tiled=True)  13.9 us
    all_to_all x2, waiting for transfers between devices, send(): return lax.all_to_all(sums.astype(jnp.bfloat16), axis, 0, 0, tiled=True)  12.5 us
    all_to_all x2, starting transfers between devices, send(): return lax.all_to_all(sums.astype(jnp.bfloat16), axis, 0, 0, tiled=True)  11.5 us
    pallas_call x1, Pallas kernels, video_grads(): pl.pallas_call(functools.partial(video_kernel, q_len=q_len, v_len=v_len,...  11.2 us
    ppermute x3, starting transfers between devices, local(): lax.ppermute(sent, 'x', [(i, (i + away) % x_count) for i in range(x_count)])  9.9 us
    pallas_call x1, Pallas kernels, caption_grads(): pl.pallas_call(caption_kernel, out_shape=tuple((jax.ShapeDtypeStruct((z_c...  5.21 us
  transfers between devices with their start and end apart: 8, of which 5 were waited for; matrix products, arithmetic and copies ran while one was open for 1% of the time, Pallas kernels for 4%

profile of v4, /device:TPU:8, one launch (start us, length us, event | category | flops | bytes accessed | tf_op | source)
XLA Modules:
  0.0 123.3 jit_solution(12851612937919254733)
XLA Ops:
  1.3 0.7 pad_bitcast_fusion
  2.0 0.7 broadcast_in_dim.38
  2.7 18.9 %all-to-all-start = ((bf16[16,40,128]{2,1,0:T(8,128)(2,1)}), bf16[16,40,128]{2,1,0:T(8,128)(2,1)S(1)}, u32[]{:S(2)}, u32[]{:S(2)}) async-start(bf16[16,40,128]{2,1,0:T(8,128)(2,1)} %broadcast_in_dim.38), calls=%async_computation | async-start | bytes 327680 | tf_op jit(solution)/shard_map/all_to_all | solution.py:162
  22.2 0.8 concatenate.7
  22.9 14.2 %all-to-all-done = bf16[16,40,128]{2,1,0:T(8,128)(2,1)S(1)} async-done(((bf16[16,40,128]{2,1,0:T(8,128)(2,1)}), bf16[16,40,128]{2,1,0:T(8,128)(2,1)S(1)}, u32[]{:S(2)}, u32[]{:S(2)}) %all-to-all-start) | async-done | bytes 163872 | tf_op jit(solution)/shard_map/all_to_all | solution.py:162
  37.2 0.7 broadcast_in_dim.41
  37.9 7.5 %all-to-all-start.1 = ((bf16[8,136,128]{2,1,0:T(8,128)(2,1)}), bf16[8,136,128]{2,1,0:T(8,128)(2,1)S(1)}, u32[]{:S(2)}, u32[]{:S(2)}) async-start(bf16[8,136,128]{2,1,0:T(8,128)(2,1)} %broadcast_in_dim.41), calls=%async_computation.1 | async-start | bytes 557056 | tf_op jit(solution)/shard_map/all_to_all | solution.py:162
  45.5 13.9 %all_gather.6.caps_ref = bf16[64,40,128]{2,1,0:T(8,128)(2,1)S(1)} all-gather(bf16[16,40,128]{2,1,0:T(8,128)(2,1)S(1)} %all-to-all-done), channel_id=1, replica_groups=mesh['z_hi'=2,'y'=8,'x'=4,'z_lo'=8,'core'=2] {'x'}, dimensions={0}, use_global_device_ids=true | all-gather | bytes 819200 | tf_op jit(solution)/shard_map/all_gather | solution.py:183
  59.3 0.0 all-to-all-done.1
  59.3 2.2 %all_gather.7.vids_ref = bf16[16,136,128]{2,1,0:T(8,128)(2,1)S(1)} all-gather(bf16[8,136,128]{2,1,0:T(8,128)(2,1)S(1)} %all-to-all-done.1), channel_id=1, replica_groups=mesh['z_hi'=2,'y'=8,'x'=4,'z_lo'=8,'core'=2] {'core'}, dimensions={0}, use_global_device_ids=true | all-gather | bytes 835584 | tf_op jit(solution)/shard_map/all_gather | solution.py:184
  61.5 11.2 %shard_map.59 = (f32[8,128,128]{2,1,0:T(8,128)S(1)}, bf16[8,128,128]{2,1,0:T(8,128)(2,1)S(1)}, bf16[128,2048]{1,0:T(8,128)(2,1)S(1)}, bf16[8,2048,256]{2,1,0:T(8,128)(2,1)}) custom-call(bf16[64,40,128]{2,1,0:T(8,128)(2,1)S(1)} %all_gather.6.caps_ref, bf16[16,136,128]{2,1,0:T(8,128)(2,1)S(1)} %all_gather.7.vids_ref), custom_call_target="tpu_custom_call" | custom-call | flops 2147483648 | bytes 8388608 | tf_op jit(solution)/shard_map/pallas_call | solution.py:112
  72.8 2.0 %collective-permute-start = (bf16[8,128,128]{2,1,0:T(8,128)(2,1)S(1)}, bf16[8,128,128]{2,1,0:T(8,128)(2,1)S(1)}, u32[]{:S(2)}, u32[]{:S(2)}) collective-permute-start(bf16[8,128,128]{2,1,0:T(8,128)(2,1)S(1)} %get-tuple-element.20), channel_id=1, source_target_pairs={{0,1},{1,0},{2,3},{3,2},{4,5},{5,4},{6,7},{7,6},{8,9},{9,8},{10,11... | collective-permute-start | bytes 786440 | tf_op jit(solution)/shard_map/ppermute | solution.py:186
  74.8 1.4 %collective-permute-done = bf16[8,128,128]{2,1,0:T(8,128)(2,1)S(1)} collective-permute-done((bf16[8,128,128]{2,1,0:T(8,128)(2,1)S(1)}, bf16[8,128,128]{2,1,0:T(8,128)(2,1)S(1)}, u32[]{:S(2)}, u32[]{:S(2)}) %collective-permute-start) | collective-permute-done | bytes 262176 | tf_op jit(solution)/shard_map/ppermute | solution.py:186
  76.2 0.8 convert_element_type.36
  77.0 7.2 %all-to-all-start.2 = ((bf16[8,128,128]{2,1,0:T(8,128)(2,1)}), bf16[8,128,128]{2,1,0:T(8,128)(2,1)S(1)}, u32[]{:S(2)}, u32[]{:S(2)}) async-start(bf16[8,128,128]{2,1,0:T(8,128)(2,1)} %convert_element_type.36), calls=%async_computation.2 | async-start | bytes 524288 | tf_op jit(solution)/shard_map/all_to_all | solution.py:166
  84.2 5.2 %shard_map.60 = (f32[16,32,128]{2,1,0:T(8,128)S(1)}, bf16[16,32,128]{2,1,0:T(8,128)(2,1)S(1)}, bf16[16,32,128]{2,1,0:T(8,128)(2,1)S(1)}, bf16[16,32,128]{2,1,0:T(8,128)(2,1)S(1)}) custom-call(bf16[8,2048,256]{2,1,0:T(8,128)(2,1)} %get-tuple-element.18.in_ref, bf16[128,2048]{1,0:T(8,128)(2,1)S(1)} %get-tuple-element.22.turned_ref), custom_call_target="tpu_custom_call" | custom-call | flops 1073741824 | bytes 8388608 | tf_op jit(solution)/shard_map/pallas_call | solution.py:137
  89.4 3.4 %collective-permute-start.1 = (bf16[16,32,128]{2,1,0:T(8,128)(2,1)S(1)}, bf16[16,32,128]{2,1,0:T(8,128)(2,1)S(1)}, u32[]{:S(2)}, u32[]{:S(2)}) collective-permute-start(bf16[16,32,128]{2,1,0:T(8,128)(2,1)S(1)} %get-tuple-element.24), channel_id=1, source_target_pairs={{0,16},{16,32},{32,48},{48,0},{1,17},{17,33},{33,49},{49,1},{2,18}... | collective-permute-start | bytes 393224 | tf_op jit(solution)/shard_map/ppermute | solution.py:191
  92.8 4.6 %collective-permute-start.2 = (bf16[16,32,128]{2,1,0:T(8,128)(2,1)S(1)}, bf16[16,32,128]{2,1,0:T(8,128)(2,1)S(1)}, u32[]{:S(2)}, u32[]{:S(2)}) collective-permute-start(bf16[16,32,128]{2,1,0:T(8,128)(2,1)S(1)} %get-tuple-element.25), channel_id=1, source_target_pairs={{0,32},{16,48},{32,0},{48,16},{1,33},{17,49},{33,1},{49,17},{2,34}... | collective-permute-start | bytes 393224 | tf_op jit(solution)/shard_map/ppermute | solution.py:191
  97.4 1.9 %collective-permute-start.3 = (bf16[16,32,128]{2,1,0:T(8,128)(2,1)S(1)}, bf16[16,32,128]{2,1,0:T(8,128)(2,1)S(1)}, u32[]{:S(2)}, u32[]{:S(2)}) collective-permute-start(bf16[16,32,128]{2,1,0:T(8,128)(2,1)S(1)} %get-tuple-element.26), channel_id=1, source_target_pairs={{0,48},{16,0},{32,16},{48,32},{1,49},{17,1},{33,17},{49,33},{2,50}... | collective-permute-start | bytes 393224 | tf_op jit(solution)/shard_map/ppermute | solution.py:191
  99.4 0.0 collective-permute-done.1
  99.4 1.9 %collective-permute-done.2 = bf16[16,32,128]{2,1,0:T(8,128)(2,1)S(1)} collective-permute-done((bf16[16,32,128]{2,1,0:T(8,128)(2,1)S(1)}, bf16[16,32,128]{2,1,0:T(8,128)(2,1)S(1)}, u32[]{:S(2)}, u32[]{:S(2)}) %collective-permute-start.2) | collective-permute-done | bytes 131104 | tf_op jit(solution)/shard_map/ppermute | solution.py:191
  101.2 3.0 %collective-permute-done.3 = bf16[16,32,128]{2,1,0:T(8,128)(2,1)S(1)} collective-permute-done((bf16[16,32,128]{2,1,0:T(8,128)(2,1)S(1)}, bf16[16,32,128]{2,1,0:T(8,128)(2,1)S(1)}, u32[]{:S(2)}, u32[]{:S(2)}) %collective-permute-start.3) | collective-permute-done | bytes 131104 | tf_op jit(solution)/shard_map/ppermute | solution.py:191
  104.3 0.1 convert_add_fusion.1
  104.3 0.0 all-to-all-done.2
  104.4 0.7 convert_element_type.37
  105.0 4.3 %all-to-all-start.3 = ((bf16[16,32,128]{2,1,0:T(8,128)(2,1)}), bf16[16,32,128]{2,1,0:T(8,128)(2,1)S(1)}, u32[]{:S(2)}, u32[]{:S(2)}) async-start(bf16[16,32,128]{2,1,0:T(8,128)(2,1)} %convert_element_type.37), calls=%async_computation.3 | async-start | bytes 262144 | tf_op jit(solution)/shard_map/all_to_all | solution.py:166
  109.4 0.1 select_reduce_fusion
  109.5 0.6 fusion
  110.1 12.5 %all-to-all-done.3 = bf16[16,32,128]{2,1,0:T(8,128)(2,1)S(1)} async-done(((bf16[16,32,128]{2,1,0:T(8,128)(2,1)}), bf16[16,32,128]{2,1,0:T(8,128)(2,1)S(1)}, u32[]{:S(2)}, u32[]{:S(2)}) %all-to-all-start.3) | async-done | bytes 131104 | tf_op jit(solution)/shard_map/all_to_all | solution.py:166
  122.6 0.1 select_reduce_fusion.1
  122.7 0.6 fusion.1
  (3 shorter events, 0.1 us)
Async XLA Ops:
  2.7 34.5 %all-to-all-start = ((bf16[16,40,128]{2,1,0:T(8,128)(2,1)}), bf16[16,40,128]{2,1,0:T(8,128)(2,1)S(1)}, u32[]{:S(2)}, u32[]{:S(2)}) async-start(bf16[16,40,128]{2,1,0:T(8,128)(2,1)} %broadcast_in_dim.38), calls=%async_computation | async-start | bytes 327680 | tf_op jit(solution)/shard_map/all_to_all | solution.py:162
  37.9 21.4 %all-to-all-start.1 = ((bf16[8,136,128]{2,1,0:T(8,128)(2,1)}), bf16[8,136,128]{2,1,0:T(8,128)(2,1)S(1)}, u32[]{:S(2)}, u32[]{:S(2)}) async-start(bf16[8,136,128]{2,1,0:T(8,128)(2,1)} %broadcast_in_dim.41), calls=%async_computation.1 | async-start | bytes 557056 | tf_op jit(solution)/shard_map/all_to_all | solution.py:162
  72.8 3.4 %collective-permute-start = (bf16[8,128,128]{2,1,0:T(8,128)(2,1)S(1)}, bf16[8,128,128]{2,1,0:T(8,128)(2,1)S(1)}, u32[]{:S(2)}, u32[]{:S(2)}) collective-permute-start(bf16[8,128,128]{2,1,0:T(8,128)(2,1)S(1)} %get-tuple-element.20), channel_id=1, source_target_pairs={{0,1},{1,0},{2,3},{3,2},{4,5},{5,4},{6,7},{7,6},{8,9},{9,8},{10,11... | collective-permute-start | bytes 786440 | tf_op jit(solution)/shard_map/ppermute | solution.py:186
  77.0 27.3 %all-to-all-start.2 = ((bf16[8,128,128]{2,1,0:T(8,128)(2,1)}), bf16[8,128,128]{2,1,0:T(8,128)(2,1)S(1)}, u32[]{:S(2)}, u32[]{:S(2)}) async-start(bf16[8,128,128]{2,1,0:T(8,128)(2,1)} %convert_element_type.36), calls=%async_computation.2 | async-start | bytes 524288 | tf_op jit(solution)/shard_map/all_to_all | solution.py:166
  89.4 9.9 %collective-permute-start.1 = (bf16[16,32,128]{2,1,0:T(8,128)(2,1)S(1)}, bf16[16,32,128]{2,1,0:T(8,128)(2,1)S(1)}, u32[]{:S(2)}, u32[]{:S(2)}) collective-permute-start(bf16[16,32,128]{2,1,0:T(8,128)(2,1)S(1)} %get-tuple-element.24), channel_id=1, source_target_pairs={{0,16},{16,32},{32,48},{48,0},{1,17},{17,33},{33,49},{49,1},{2,18}... | collective-permute-start | bytes 393224 | tf_op jit(solution)/shard_map/ppermute | solution.py:191
  92.8 8.4 %collective-permute-start.2 = (bf16[16,32,128]{2,1,0:T(8,128)(2,1)S(1)}, bf16[16,32,128]{2,1,0:T(8,128)(2,1)S(1)}, u32[]{:S(2)}, u32[]{:S(2)}) collective-permute-start(bf16[16,32,128]{2,1,0:T(8,128)(2,1)S(1)} %get-tuple-element.25), channel_id=1, source_target_pairs={{0,32},{16,48},{32,0},{48,16},{1,33},{17,49},{33,1},{49,17},{2,34}... | collective-permute-start | bytes 393224 | tf_op jit(solution)/shard_map/ppermute | solution.py:191
  97.4 6.9 %collective-permute-start.3 = (bf16[16,32,128]{2,1,0:T(8,128)(2,1)S(1)}, bf16[16,32,128]{2,1,0:T(8,128)(2,1)S(1)}, u32[]{:S(2)}, u32[]{:S(2)}) collective-permute-start(bf16[16,32,128]{2,1,0:T(8,128)(2,1)S(1)} %get-tuple-element.26), channel_id=1, source_target_pairs={{0,48},{16,0},{32,16},{48,32},{1,49},{17,1},{33,17},{49,33},{2,50}... | collective-permute-start | bytes 393224 | tf_op jit(solution)/shard_map/ppermute | solution.py:191
  105.0 17.6 %all-to-all-start.3 = ((bf16[16,32,128]{2,1,0:T(8,128)(2,1)}), bf16[16,32,128]{2,1,0:T(8,128)(2,1)S(1)}, u32[]{:S(2)}, u32[]{:S(2)}) async-start(bf16[16,32,128]{2,1,0:T(8,128)(2,1)} %convert_element_type.37), calls=%async_computation.3 | async-start | bytes 262144 | tf_op jit(solution)/shard_map/all_to_all | solution.py:166

commit v5 on v3

--- a/solution.py
+++ b/solution.py
@@ -34,8 +34,7 @@
     def queries_of(block):
         return caps_ref[pl.ds(block * block_caps, block_caps), :q_len, :].reshape(lanes, features)
 
-    @pl.loop(0, blocks)
-    def _(block):
+    def score(block):
         queries = queries_of(block)
         for v in range(vid_rows):
             scores = lax.dot_general(
@@ -57,8 +56,7 @@
 
     mine_ref[...] = jnp.zeros_like(mine_ref)
 
-    @pl.loop(0, blocks)
-    def _(block):
+    def scale(block):
         summed = sum_ref[block]
         pooled = peak_ref[block] + pool_tau * jnp.log(summed)
         logits = jnp.dot(pooled, spread, preferred_element_type=jnp.float32, precision=lax.Precision.HIGHEST)
@@ -69,12 +67,11 @@
             row_norm = jnp.where(lane_cap[:1] == c, norm, row_norm)
         paired = (lane_cap + block * block_caps == own_cap) & (sub_vid == own_vid)
         pair_grad = (jnp.exp(logits - row_norm) + jnp.exp(logits - col_norm) - 2.0 * paired.astype(jnp.float32)) / (2.0 * logit_temp)
-        scale = pair_grad / (summed * q_len)
-        sum_ref[block] = jnp.where(paired, 0.0, scale)
-        mine_ref[...] += jnp.where(paired, scale, 0.0)
+        factor = pair_grad / (summed * q_len)
+        sum_ref[block] = jnp.where(paired, 0.0, factor)
+        mine_ref[...] += jnp.where(paired, factor, 0.0)
 
-    @pl.loop(0, blocks)
-    def _(block):
+    def multiply(block):
         queries = queries_of(block)
         for v in range(vid_rows):
             coef_ref[pl.ds(v * v_len, v_len), :] = (lift_ref[block, v] * sum_ref[block, pl.ds(v, 1), :]).astype(jnp.bfloat16)
@@ -82,6 +79,14 @@
         turned = jnp.dot(turned_ref[...], coef, preferred_element_type=jnp.float32)
         dq_ref[pl.ds(block * block_caps, block_caps)] = turned.T.reshape(block_caps, q_len, features).astype(dq_ref.dtype)
         total_ref[...] += jnp.dot(coef, queries, preferred_element_type=jnp.float32)
+
+    score(0)
+    scale(0)
+    for block in range(1, blocks):
+        score(block)
+        multiply(block - 1)
+        scale(block)
+    multiply(blocks - 1)
 
     own_scale = jnp.sum(mine_ref[...], axis=0, keepdims=True)
     coef = (lift_ref[own_block, own_vid] * own_scale).astype(jnp.bfloat16)
@@ -150,6 +155,18 @@
     return jnp.sum(moved.astype(jnp.float32), axis=0)
 
 
+def halve(kept, sent, axis, bit):
+    across = [(i, i ^ (1 << bit)) for i in range(lax.axis_size(axis))]
+    return kept + lax.ppermute(sent, axis, across).astype(jnp.float32)
+
+
+def sum_over_bit(kept, axis, bit, dtype):
+    kept = kept.reshape(-1, 2, *kept.shape[1:])
+    own = (lax.axis_index(axis) >> bit) & 1
+    sent = lax.dynamic_index_in_dim(kept, 1 - own, 1, keepdims=False).astype(dtype)
+    return halve(lax.dynamic_index_in_dim(kept, own, 1, keepdims=False), sent, axis, bit)
+
+
 def local(caption_tokens, video_tokens, row_norms, col_norms):
     q_len, v_len, features = caption_tokens.shape[1], video_tokens.shape[1], caption_tokens.shape[2]
     x_count, z_count = lax.axis_size("x"), lax.axis_size(Z)
@@ -160,9 +177,13 @@
     caps = lax.all_gather(caps, "x", axis=0, tiled=True)
     vids = lax.all_gather(vids, "core", axis=0, tiled=True)
     dq, own_dq, dv_kept, dv_sent = pair_grads(caps, vids, q_len, v_len)
-    dv = dv_kept + lax.ppermute(dv_sent, "core", [(0, 1), (1, 0)]).astype(jnp.float32)
-    dv = lax.psum_scatter(dv, "y", scatter_dimension=0, tiled=False).astype(jnp.bfloat16)
     dq = sum_over(dq.reshape(x_count, z_count, q_len, features), "x").astype(jnp.bfloat16)
+    dv = halve(dv_kept, dv_sent, "core", 0)
+    last = lax.axis_size("y").bit_length() - 2
+    for bit in range(last):
+        dv = sum_over_bit(dv, "y", bit, jnp.bfloat16)
+    dq, dv = lax.optimization_barrier((dq, dv))
+    dv = sum_over_bit(dv, "y", last, jnp.float32)[0].astype(jnp.bfloat16)
     dq = (sum_over(dq, Z) + own_dq).astype(jnp.bfloat16)
     return dq[None], dv[None]
 

time: 139 us -> 111 us (0.80)
  the two profiles are of different devices: /device:TPU:8 before, /device:TPU:16 now
where the time goes in v5:
time: 111 us
  starting transfers between devices  46.7 us (42%)
  waiting for transfers between devices  32.6 us (29%)
  blocking collectives  16.1 us (15%)
  Pallas kernels  9 us (8%)
  local copies, waits for them, and re-layouts  2.18 us (2%)
  other arithmetic  2.08 us (2%)
  between operations  2.07 us (2%)
    all_to_all x2, starting transfers between devices, spread_over(): return lax.all_to_all(copies, axis, 0, 0, tiled=True)  26.4 us
    all_to_all x2, waiting for transfers between devices, spread_over(): return lax.all_to_all(copies, axis, 0, 0, tiled=True)  15 us
    all_gather x1, blocking collectives, local(): caps = lax.all_gather(caps, 'x', axis=0, tiled=True)  13.9 us
    ppermute x4, starting transfers between devices, halve(): return kept + lax.ppermute(sent, axis, across).astype(jnp.float32)  12.4 us
    all_to_all x2, waiting for transfers between devices, sum_over(): moved = lax.all_to_all(parts, axis, 0, 0, tiled=True)  9.79 us
    pallas_call x1, Pallas kernels, pair_grads(): pl.pallas_call(functools.partial(pair_kernel, q_len=q_len, v_len=v_len, l...  9 us
    all_to_all x2, starting transfers between devices, sum_over(): moved = lax.all_to_all(parts, axis, 0, 0, tiled=True)  7.86 us
    ppermute x4, waiting for transfers between devices, halve(): return kept + lax.ppermute(sent, axis, across).astype(jnp.float32)  7.8 us
  transfers between devices with their start and end apart: 8, of which 6 were waited for; matrix products, arithmetic and copies ran while one was open for 1% of the time, Pallas kernels for 0%

profile of v5, /device:TPU:16, one launch (start us, length us, event | category | flops | bytes accessed | tf_op | source)
XLA Modules:
  0.0 110.7 jit_solution(15421147270340088403)
XLA Ops:
  1.3 0.7 pad_bitcast_fusion
  2.0 0.7 broadcast_in_dim.32
  2.7 0.0 copy-start
  2.7 19.0 %all-to-all-start = ((bf16[16,40,128]{2,1,0:T(8,128)(2,1)}), bf16[16,40,128]{2,1,0:T(8,128)(2,1)S(1)}, u32[]{:S(2)}, u32[]{:S(2)}) async-start(bf16[16,40,128]{2,1,0:T(8,128)(2,1)} %broadcast_in_dim.32), calls=%async_computation | async-start | bytes 327680 | tf_op jit(solution)/shard_map/all_to_all | solution.py:150
  22.3 0.0 copy-done
  22.3 15.0 %all-to-all-done = bf16[16,40,128]{2,1,0:T(8,128)(2,1)S(1)} async-done(((bf16[16,40,128]{2,1,0:T(8,128)(2,1)}), bf16[16,40,128]{2,1,0:T(8,128)(2,1)S(1)}, u32[]{:S(2)}, u32[]{:S(2)}) %all-to-all-start) | async-done | bytes 163872 | tf_op jit(solution)/shard_map/all_to_all | solution.py:150
  37.3 0.7 broadcast_in_dim.35
  38.0 7.4 %all-to-all-start.1 = ((bf16[8,136,128]{2,1,0:T(8,128)(2,1)}), bf16[8,136,128]{2,1,0:T(8,128)(2,1)S(1)}, u32[]{:S(2)}, u32[]{:S(2)}) async-start(bf16[8,136,128]{2,1,0:T(8,128)(2,1)} %broadcast_in_dim.35), calls=%async_computation.1 | async-start | bytes 557056 | tf_op jit(solution)/shard_map/all_to_all | solution.py:150
  45.5 13.9 %all_gather.6.caps_ref = bf16[64,40,128]{2,1,0:T(8,128)(2,1)S(1)} all-gather(bf16[16,40,128]{2,1,0:T(8,128)(2,1)S(1)} %all-to-all-done), channel_id=1, replica_groups=mesh['z_hi'=2,'y'=8,'x'=4,'z_lo'=8,'core'=2] {'x'}, dimensions={0}, use_global_device_ids=true | all-gather | bytes 819200 | tf_op jit(solution)/shard_map/all_gather | solution.py:177
  59.4 0.0 all-to-all-done.1
  59.4 2.2 %all_gather.7.vids_ref = bf16[16,136,128]{2,1,0:T(8,128)(2,1)S(1)} all-gather(bf16[8,136,128]{2,1,0:T(8,128)(2,1)S(1)} %all-to-all-done.1), channel_id=1, replica_groups=mesh['z_hi'=2,'y'=8,'x'=4,'z_lo'=8,'core'=2] {'core'}, dimensions={0}, use_global_device_ids=true | all-gather | bytes 835584 | tf_op jit(solution)/shard_map/all_gather | solution.py:178
  61.6 9.0 %shard_map.59 = (bf16[64,32,128]{2,1,0:T(8,128)(2,1)}, f32[32,128]{1,0:T(8,128)S(1)}, f32[8,128,128]{2,1,0:T(8,128)S(1)}, bf16[8,128,128]{2,1,0:T(8,128)(2,1)S(1)}) custom-call(bf16[64,40,128]{2,1,0:T(8,128)(2,1)S(1)} %all_gather.6.caps_ref, bf16[16,136,128]{2,1,0:T(8,128)(2,1)S(1)} %all_gather.7.vids_ref), custom_call_target="tpu_custom_call" | custom-call | flops 3221225472 | bytes 2097152 | tf_op jit(solution)/shard_map/pallas_call | solution.py:107
  70.5 2.0 %collective-permute-start = (bf16[8,128,128]{2,1,0:T(8,128)(2,1)S(1)}, bf16[8,128,128]{2,1,0:T(8,128)(2,1)S(1)}, u32[]{:S(2)}, u32[]{:S(2)}) collective-permute-start(bf16[8,128,128]{2,1,0:T(8,128)(2,1)S(1)} %get-tuple-element.14), channel_id=1, source_target_pairs={{0,1},{1,0},{2,3},{3,2},{4,5},{5,4},{6,7},{7,6},{8,9},{9,8},{10,11... | collective-permute-start | bytes 786440 | tf_op jit(solution)/shard_map/ppermute | solution.py:160
  72.6 1.4 %collective-permute-done = bf16[8,128,128]{2,1,0:T(8,128)(2,1)S(1)} collective-permute-done((bf16[8,128,128]{2,1,0:T(8,128)(2,1)S(1)}, bf16[8,128,128]{2,1,0:T(8,128)(2,1)S(1)}, u32[]{:S(2)}, u32[]{:S(2)}) %collective-permute-start) | collective-permute-done | bytes 262176 | tf_op jit(solution)/shard_map/ppermute | solution.py:160
  74.1 3.7 %collective-permute-start.1 = (bf16[4,128,128]{2,1,0:T(8,128)(2,1)S(1)}, bf16[4,128,128]{2,1,0:T(8,128)(2,1)S(1)}, u32[]{:S(2)}, u32[]{:S(2)}) collective-permute-start(bf16[4,128,128]{2,1,0:T(8,128)(2,1)S(1)} %fusion), channel_id=1, source_target_pairs={{0,64},{64,0},{128,192},{192,128},{256,320},{320,256},{384,448},{4... | collective-permute-start | bytes 393224 | tf_op jit(solution)/shard_map/ppermute | solution.py:160
  77.7 3.5 %all-to-all-start.2 = ((bf16[4,16,32,128]{3,2,1,0:T(8,128)(2,1)}), bf16[4,16,32,128]{3,2,1,0:T(8,128)(2,1)S(1)}, u32[]{:S(2)}, u32[]{:S(2)}) async-start(bf16[4,16,32,128]{3,2,1,0:T(8,128)(2,1)} %bitcast.4), calls=%async_computation.2 | async-start | bytes 1048576 | tf_op jit(solution)/shard_map/all_to_all | solution.py:154
  81.3 0.2 collective-permute-done.1
  81.6 2.2 %collective-permute-start.2 = (bf16[2,128,128]{2,1,0:T(8,128)(2,1)S(1)}, bf16[2,128,128]{2,1,0:T(8,128)(2,1)S(1)}, u32[]{:S(2)}, u32[]{:S(2)}) collective-permute-start(bf16[2,128,128]{2,1,0:T(8,128)(2,1)S(1)} %fusion.1), channel_id=1, source_target_pairs={{0,128},{64,192},{128,0},{192,64},{256,384},{320,448},{384,256},{4... | collective-permute-start | bytes 196616 | tf_op jit(solution)/shard_map/ppermute | solution.py:160
  83.8 7.2 %all-to-all-done.2 = bf16[4,16,32,128]{3,2,1,0:T(8,128)(2,1)S(1)} async-done(((bf16[4,16,32,128]{3,2,1,0:T(8,128)(2,1)}), bf16[4,16,32,128]{3,2,1,0:T(8,128)(2,1)S(1)}, u32[]{:S(2)}, u32[]{:S(2)}) %all-to-all-start.2) | async-done | bytes 524320 | tf_op jit(solution)/shard_map/all_to_all | solution.py:154
  91.0 0.7 reduce_sum.21
  91.7 0.0 collective-permute-done.2
  91.7 4.3 %all-to-all-start.3 = ((bf16[16,32,128]{2,1,0:T(8,128)(2,1)}), bf16[16,32,128]{2,1,0:T(8,128)(2,1)S(1)}, u32[]{:S(2)}, u32[]{:S(2)}) async-start(bf16[16,32,128]{2,1,0:T(8,128)(2,1)} %reduce_sum.21), calls=%async_computation.3 | async-start | bytes 262144 | tf_op jit(solution)/shard_map/all_to_all | solution.py:154
  96.1 4.6 %collective-permute-start.3 = (f32[1,128,128]{2,1,0:T(8,128)S(1)}, f32[1,128,128]{2,1,0:T(8,128)S(1)}, u32[]{:S(2)}, u32[]{:S(2)}) collective-permute-start(f32[1,128,128]{2,1,0:T(8,128)S(1)} %constant_dynamic-slice_fusion), channel_id=1, source_target_pairs={{0,256},{64,320},{128,384},{192,448},{256,0},{320,64},{384,128},{4... | collective-permute-start | bytes 196616 | tf_op jit(solution)/shard_map/ppermute | solution.py:160
  100.7 6.2 %collective-permute-done.3 = f32[1,128,128]{2,1,0:T(8,128)S(1)} collective-permute-done((f32[1,128,128]{2,1,0:T(8,128)S(1)}, f32[1,128,128]{2,1,0:T(8,128)S(1)}, u32[]{:S(2)}, u32[]{:S(2)}) %collective-permute-start.3) | collective-permute-done | bytes 65568 | tf_op jit(solution)/shard_map/ppermute | solution.py:160
  106.8 0.6 add_convert_fusion
  107.5 2.6 %all-to-all-done.3 = bf16[16,32,128]{2,1,0:T(8,128)(2,1)S(1)} async-done(((bf16[16,32,128]{2,1,0:T(8,128)(2,1)}), bf16[16,32,128]{2,1,0:T(8,128)(2,1)S(1)}, u32[]{:S(2)}, u32[]{:S(2)}) %all-to-all-start.3) | async-done | bytes 131104 | tf_op jit(solution)/shard_map/all_to_all | solution.py:154
  110.1 0.6 fusion.2
  (8 shorter events, 0.2 us)
Async XLA Ops:
  2.7 19.7 %copy-start = (bf16[1,128,128]{2,1,0:T(8,128)(2,1)S(1)}, bf16[1,128,128]{2,1,0:T(8,128)(2,1)}, u32[]{:S(2)}) copy-start(bf16[1,128,128]{2,1,0:T(8,128)(2,1)} %param.5) | copy-start | bytes 98308
  2.7 34.6 %all-to-all-start = ((bf16[16,40,128]{2,1,0:T(8,128)(2,1)}), bf16[16,40,128]{2,1,0:T(8,128)(2,1)S(1)}, u32[]{:S(2)}, u32[]{:S(2)}) async-start(bf16[16,40,128]{2,1,0:T(8,128)(2,1)} %broadcast_in_dim.32), calls=%async_computation | async-start | bytes 327680 | tf_op jit(solution)/shard_map/all_to_all | solution.py:150
  38.0 21.3 %all-to-all-start.1 = ((bf16[8,136,128]{2,1,0:T(8,128)(2,1)}), bf16[8,136,128]{2,1,0:T(8,128)(2,1)S(1)}, u32[]{:S(2)}, u32[]{:S(2)}) async-start(bf16[8,136,128]{2,1,0:T(8,128)(2,1)} %broadcast_in_dim.35), calls=%async_computation.1 | async-start | bytes 557056 | tf_op jit(solution)/shard_map/all_to_all | solution.py:150
  70.5 3.4 %collective-permute-start = (bf16[8,128,128]{2,1,0:T(8,128)(2,1)S(1)}, bf16[8,128,128]{2,1,0:T(8,128)(2,1)S(1)}, u32[]{:S(2)}, u32[]{:S(2)}) collective-permute-start(bf16[8,128,128]{2,1,0:T(8,128)(2,1)S(1)} %get-tuple-element.14), channel_id=1, source_target_pairs={{0,1},{1,0},{2,3},{3,2},{4,5},{5,4},{6,7},{7,6},{8,9},{9,8},{10,11... | collective-permute-start | bytes 786440 | tf_op jit(solution)/shard_map/ppermute | solution.py:160
  74.1 7.5 %collective-permute-start.1 = (bf16[4,128,128]{2,1,0:T(8,128)(2,1)S(1)}, bf16[4,128,128]{2,1,0:T(8,128)(2,1)S(1)}, u32[]{:S(2)}, u32[]{:S(2)}) collective-permute-start(bf16[4,128,128]{2,1,0:T(8,128)(2,1)S(1)} %fusion), channel_id=1, source_target_pairs={{0,64},{64,0},{128,192},{192,128},{256,320},{320,256},{384,448},{4... | collective-permute-start | bytes 393224 | tf_op jit(solution)/shard_map/ppermute | solution.py:160
  77.7 13.2 %all-to-all-start.2 = ((bf16[4,16,32,128]{3,2,1,0:T(8,128)(2,1)}), bf16[4,16,32,128]{3,2,1,0:T(8,128)(2,1)S(1)}, u32[]{:S(2)}, u32[]{:S(2)}) async-start(bf16[4,16,32,128]{3,2,1,0:T(8,128)(2,1)} %bitcast.4), calls=%async_computation.2 | async-start | bytes 1048576 | tf_op jit(solution)/shard_map/all_to_all | solution.py:154
  81.6 10.1 %collective-permute-start.2 = (bf16[2,128,128]{2,1,0:T(8,128)(2,1)S(1)}, bf16[2,128,128]{2,1,0:T(8,128)(2,1)S(1)}, u32[]{:S(2)}, u32[]{:S(2)}) collective-permute-start(bf16[2,128,128]{2,1,0:T(8,128)(2,1)S(1)} %fusion.1), channel_id=1, source_target_pairs={{0,128},{64,192},{128,0},{192,64},{256,384},{320,448},{384,256},{4... | collective-permute-start | bytes 196616 | tf_op jit(solution)/shard_map/ppermute | solution.py:160
  91.7 18.3 %all-to-all-start.3 = ((bf16[16,32,128]{2,1,0:T(8,128)(2,1)}), bf16[16,32,128]{2,1,0:T(8,128)(2,1)S(1)}, u32[]{:S(2)}, u32[]{:S(2)}) async-start(bf16[16,32,128]{2,1,0:T(8,128)(2,1)} %reduce_sum.21), calls=%async_computation.3 | async-start | bytes 262144 | tf_op jit(solution)/shard_map/all_to_all | solution.py:154
  96.1 10.8 %collective-permute-start.3 = (f32[1,128,128]{2,1,0:T(8,128)S(1)}, f32[1,128,128]{2,1,0:T(8,128)S(1)}, u32[]{:S(2)}, u32[]{:S(2)}) collective-permute-start(f32[1,128,128]{2,1,0:T(8,128)S(1)} %constant_dynamic-slice_fusion), channel_id=1, source_target_pairs={{0,256},{64,320},{128,384},{192,448},{256,0},{320,64},{384,128},{4... | collective-permute-start | bytes 196616 | tf_op jit(solution)/shard_map/ppermute | solution.py:160

commit v6 on v5

--- a/solution.py
+++ b/solution.py
@@ -24,7 +24,7 @@
     to_exp2 = 1.0 / (pool_tau * math.log(2.0))
 
     own_cap = lax.axis_index("x") * lax.axis_size(Z) + lax.axis_index("z_hi") * lax.axis_size("z_lo") + lax.axis_index("z_lo")
-    own_vid = lax.axis_index("core") * lax.axis_size("y") + lax.axis_index("y")
+    own_vid = lax.axis_index("y") * lax.axis_size("core") + lax.axis_index("core")
     cap_bits = block_caps.bit_length() - 1
     own_block, own_place = own_cap >> cap_bits, own_cap & (block_caps - 1)
 
@@ -91,10 +91,13 @@
     own_scale = jnp.sum(mine_ref[...], axis=0, keepdims=True)
     coef = (lift_ref[own_block, own_vid] * own_scale).astype(jnp.bfloat16)
     total_ref[pl.ds(own_vid * v_len, v_len), :] += jnp.dot(coef, queries_of(own_block), preferred_element_type=jnp.float32)
-    half = vid_rows // 2 * v_len
-    core = lax.axis_index("core")
-    dv_kept_ref[...] = total_ref[pl.ds(core * half, half), :].reshape(dv_kept_ref.shape)
-    dv_sent_ref[...] = total_ref[pl.ds((1 - core) * half, half), :].reshape(dv_sent_ref.shape).astype(dv_sent_ref.dtype)
+    bit = lax.axis_index("y") & 1
+    y_half = lax.axis_size("y") // 2
+    for pair in range(vid_rows // 2):
+        core, high = divmod(pair, y_half)
+        kept_at, sent_at = (4 * high + 2 * bit + core) * v_len, (4 * high + 2 - 2 * bit + core) * v_len
+        dv_kept_ref[pair] = total_ref[pl.ds(pl.multiple_of(kept_at, v_len), v_len), :]
+        dv_sent_ref[pair] = total_ref[pl.ds(pl.multiple_of(sent_at, v_len), v_len), :].astype(dv_sent_ref.dtype)
     total_ref[pl.ds(0, lanes), :] = lax.dot_general(
         coef, vids_ref[own_vid, :v_len, :], (((0,), (0,)), ((), ())), preferred_element_type=jnp.float32
     )
@@ -144,15 +147,16 @@
     return jnp.concatenate([tokens, jnp.broadcast_to(norm[:, None, None], (1, 8, tokens.shape[2]))], axis=1)
 
 
-def spread_over(block, axis):
-    size = lax.axis_size(axis)
-    copies = jnp.broadcast_to(block[None], (size, *block.shape))
-    return lax.all_to_all(copies, axis, 0, 0, tiled=True)
+def copies(block, count):
+    return jnp.broadcast_to(block[None], (count, *block.shape))
+
+
+def send(parts, axis):
+    return lax.all_to_all(parts, axis, 0, 0, tiled=True)
 
 
 def sum_over(parts, axis):
-    moved = lax.all_to_all(parts, axis, 0, 0, tiled=True)
-    return jnp.sum(moved.astype(jnp.float32), axis=0)
+    return jnp.sum(send(parts, axis).astype(jnp.float32), axis=0)
 
 
 def halve(kept, sent, axis, bit):
@@ -170,20 +174,21 @@
 def local(caption_tokens, video_tokens, row_norms, col_norms):
     q_len, v_len, features = caption_tokens.shape[1], video_tokens.shape[1], caption_tokens.shape[2]
     x_count, z_count = lax.axis_size("x"), lax.axis_size(Z)
-    caps = spread_over(with_norm(caption_tokens, row_norms)[0], Z)
-    vids = with_norm(video_tokens, col_norms)
+    caps = send(copies(with_norm(caption_tokens, row_norms)[0], z_count), Z)
+    vids = lax.all_gather(with_norm(video_tokens, col_norms), "core", axis=0, tiled=True)
+    vids = copies(vids, lax.axis_size("y"))
     caps, vids = lax.optimization_barrier((caps, vids))
-    vids = spread_over(vids[0], "y")
+    vids = send(vids, "y").reshape(-1, *vids.shape[2:])
     caps = lax.all_gather(caps, "x", axis=0, tiled=True)
-    vids = lax.all_gather(vids, "core", axis=0, tiled=True)
     dq, own_dq, dv_kept, dv_sent = pair_grads(caps, vids, q_len, v_len)
     dq = sum_over(dq.reshape(x_count, z_count, q_len, features), "x").astype(jnp.bfloat16)
-    dv = halve(dv_kept, dv_sent, "core", 0)
+    dv = halve(dv_kept, dv_sent, "y", 0)
     last = lax.axis_size("y").bit_length() - 2
-    for bit in range(last):
+    for bit in range(1, last):
         dv = sum_over_bit(dv, "y", bit, jnp.bfloat16)
     dq, dv = lax.optimization_barrier((dq, dv))
-    dv = sum_over_bit(dv, "y", last, jnp.float32)[0].astype(jnp.bfloat16)
+    dv = sum_over_bit(dv, "y", last, jnp.bfloat16)
+    dv = sum_over_bit(dv, "core", 0, jnp.float32)[0].astype(jnp.bfloat16)
     dq = (sum_over(dq, Z) + own_dq).astype(jnp.bfloat16)
     return dq[None], dv[None]
 

time: 111 us -> 114 us (1.027)
  the two profiles are of different devices: /device:TPU:16 before, /device:TPU:2 now
where the time goes in v6:
time: 114 us
  starting transfers between devices  49.9 us (44%)
  waiting for transfers between devices  32.4 us (28%)
  blocking collectives  15.7 us (14%)
  Pallas kernels  9.01 us (8%)
  local copies, waits for them, and re-layouts  2.32 us (2%)
  other arithmetic  2.08 us (2%)
  between operations  2.08 us (2%)
    all_to_all x4, starting transfers between devices, send(): return lax.all_to_all(parts, axis, 0, 0, tiled=True)  35.1 us
    all_to_all x4, waiting for transfers between devices, send(): return lax.all_to_all(parts, axis, 0, 0, tiled=True)  23.7 us
    ppermute x4, starting transfers between devices, halve(): return kept + lax.ppermute(sent, axis, across).astype(jnp.float32)  14.9 us
    all_gather x1, blocking collectives, local(): caps = lax.all_gather(caps, 'x', axis=0, tiled=True)  13.9 us
    pallas_call x1, Pallas kernels, pair_grads(): pl.pallas_call(functools.partial(pair_kernel, q_len=q_len, v_len=v_len, l...  9.01 us
    ppermute x4, waiting for transfers between devices, halve(): return kept + lax.ppermute(sent, axis, across).astype(jnp.float32)  8.75 us
  transfers between devices with their start and end apart: 8, of which 7 were waited for; matrix products, arithmetic and copies ran while one was open for 1% of the time, Pallas kernels for 0%

profile of v6, /device:TPU:2, one launch (start us, length us, event | category | flops | bytes accessed | tf_op | source)
XLA Modules:
  0.0 113.6 jit_solution(12641657207649722648)
XLA Ops:
  1.3 0.7 pad_bitcast_fusion
  2.0 0.7 broadcast_in_dim.14
  2.7 0.0 copy-start
  2.7 19.0 %all-to-all-start = ((bf16[16,40,128]{2,1,0:T(8,128)(2,1)}), bf16[16,40,128]{2,1,0:T(8,128)(2,1)S(1)}, u32[]{:S(2)}, u32[]{:S(2)}) async-start(bf16[16,40,128]{2,1,0:T(8,128)(2,1)} %broadcast_in_dim.14), calls=%async_computation | async-start | bytes 327680 | tf_op jit(solution)/shard_map/all_to_all | solution.py:155
  22.3 0.0 copy-done
  22.3 1.9 %all_gather.6 = bf16[2,136,128]{2,1,0:T(8,128)(2,1)S(1)} all-gather(bf16[1,136,128]{2,1,0:T(8,128)(2,1)S(1)} %concatenate.7), channel_id=1, replica_groups=mesh['z_hi'=2,'y'=8,'x'=4,'z_lo'=8,'core'=2] {'core'}, dimensions={0}, use_global_device_ids=true | all-gather | bytes 104448 | tf_op jit(solution)/shard_map/all_gather | solution.py:178
  24.2 13.1 %all-to-all-done = bf16[16,40,128]{2,1,0:T(8,128)(2,1)S(1)} async-done(((bf16[16,40,128]{2,1,0:T(8,128)(2,1)}), bf16[16,40,128]{2,1,0:T(8,128)(2,1)S(1)}, u32[]{:S(2)}, u32[]{:S(2)}) %all-to-all-start) | async-done | bytes 163872 | tf_op jit(solution)/shard_map/all_to_all | solution.py:155
  37.3 0.9 broadcast_in_dim.16
  38.2 7.1 %all-to-all-start.1 = ((bf16[8,2,136,128]{3,2,1,0:T(8,128)(2,1)}), bf16[8,2,136,128]{3,2,1,0:T(8,128)(2,1)S(1)}, u32[]{:S(2)}, u32[]{:S(2)}) async-start(bf16[8,2,136,128]{3,2,1,0:T(8,128)(2,1)} %broadcast_in_dim.16), calls=%async_computation.1 | async-start | bytes 1114112 | tf_op jit(solution)/shard_map/all_to_all | solution.py:155
  45.3 13.9 %all_gather.7.caps_ref = bf16[64,40,128]{2,1,0:T(8,128)(2,1)S(1)} all-gather(bf16[16,40,128]{2,1,0:T(8,128)(2,1)S(1)} %all-to-all-done), channel_id=1, replica_groups=mesh['z_hi'=2,'y'=8,'x'=4,'z_lo'=8,'core'=2] {'x'}, dimensions={0}, use_global_device_ids=true | all-gather | bytes 819200 | tf_op jit(solution)/shard_map/all_gather | solution.py:182
  59.1 0.6 all-to-all-done.1
  59.8 9.0 %shard_map.59 = (bf16[64,32,128]{2,1,0:T(8,128)(2,1)}, f32[32,128]{1,0:T(8,128)S(1)}, f32[8,128,128]{2,1,0:T(8,128)S(1)}, bf16[8,128,128]{2,1,0:T(8,128)(2,1)S(1)}) custom-call(bf16[64,40,128]{2,1,0:T(8,128)(2,1)S(1)} %all_gather.7.caps_ref, bf16[16,136,128]{2,1,0:T(8,128)(2,1)S(1)} %bitcast.24), custom_call_target="tpu_custom_call" | custom-call | flops 3221225472 | bytes 2097152 | tf_op jit(solution)/shard_map/pallas_call | solution.py:110
  68.8 3.0 %collective-permute-start = (bf16[8,128,128]{2,1,0:T(8,128)(2,1)S(1)}, bf16[8,128,128]{2,1,0:T(8,128)(2,1)S(1)}, u32[]{:S(2)}, u32[]{:S(2)}) collective-permute-start(bf16[8,128,128]{2,1,0:T(8,128)(2,1)S(1)} %get-tuple-element.14), channel_id=1, source_target_pairs={{0,64},{64,0},{128,192},{192,128},{256,320},{320,256},{384,448},{4... | collective-permute-start | bytes 786440 | tf_op jit(solution)/shard_map/ppermute | solution.py:164
  71.8 4.5 %all-to-all-start.2 = ((bf16[4,16,32,128]{3,2,1,0:T(8,128)(2,1)}), bf16[4,16,32,128]{3,2,1,0:T(8,128)(2,1)S(1)}, u32[]{:S(2)}, u32[]{:S(2)}) async-start(bf16[4,16,32,128]{3,2,1,0:T(8,128)(2,1)} %bitcast.4), calls=%async_computation.2 | async-start | bytes 1048576 | tf_op jit(solution)/shard_map/all_to_all | solution.py:155
  76.3 2.1 %collective-permute-done = bf16[8,128,128]{2,1,0:T(8,128)(2,1)S(1)} collective-permute-done((bf16[8,128,128]{2,1,0:T(8,128)(2,1)S(1)}, bf16[8,128,128]{2,1,0:T(8,128)(2,1)S(1)}, u32[]{:S(2)}, u32[]{:S(2)}) %collective-permute-start) | collective-permute-done | bytes 262176 | tf_op jit(solution)/shard_map/ppermute | solution.py:164
  78.5 4.0 %collective-permute-start.1 = (bf16[4,128,128]{2,1,0:T(8,128)(2,1)S(1)}, bf16[4,128,128]{2,1,0:T(8,128)(2,1)S(1)}, u32[]{:S(2)}, u32[]{:S(2)}) collective-permute-start(bf16[4,128,128]{2,1,0:T(8,128)(2,1)S(1)} %fusion), channel_id=1, source_target_pairs={{0,128},{64,192},{128,0},{192,64},{256,384},{320,448},{384,256},{4... | collective-permute-start | bytes 393224 | tf_op jit(solution)/shard_map/ppermute | solution.py:164
  82.5 0.4 all-to-all-done.2
  83.0 0.7 reduce_sum.21
  83.7 5.4 %collective-permute-done.1 = bf16[4,128,128]{2,1,0:T(8,128)(2,1)S(1)} collective-permute-done((bf16[4,128,128]{2,1,0:T(8,128)(2,1)S(1)}, bf16[4,128,128]{2,1,0:T(8,128)(2,1)S(1)}, u32[]{:S(2)}, u32[]{:S(2)}) %collective-permute-start.1) | collective-permute-done | bytes 131104 | tf_op jit(solution)/shard_map/ppermute | solution.py:164
  89.2 6.0 %collective-permute-start.2 = (bf16[2,128,128]{2,1,0:T(8,128)(2,1)S(1)}, bf16[2,128,128]{2,1,0:T(8,128)(2,1)S(1)}, u32[]{:S(2)}, u32[]{:S(2)}) collective-permute-start(bf16[2,128,128]{2,1,0:T(8,128)(2,1)S(1)} %fusion.1), channel_id=1, source_target_pairs={{0,256},{64,320},{128,384},{192,448},{256,0},{320,64},{384,128},{4... | collective-permute-start | bytes 196616 | tf_op jit(solution)/shard_map/ppermute | solution.py:164
  95.2 4.4 %all-to-all-start.3 = ((bf16[16,32,128]{2,1,0:T(8,128)(2,1)}), bf16[16,32,128]{2,1,0:T(8,128)(2,1)S(1)}, u32[]{:S(2)}, u32[]{:S(2)}) async-start(bf16[16,32,128]{2,1,0:T(8,128)(2,1)} %reduce_sum.21), calls=%async_computation.3 | async-start | bytes 262144 | tf_op jit(solution)/shard_map/all_to_all | solution.py:155
  99.6 0.0 collective-permute-done.2
  99.7 1.9 %collective-permute-start.3 = (f32[1,128,128]{2,1,0:T(8,128)S(1)}, f32[1,128,128]{2,1,0:T(8,128)S(1)}, u32[]{:S(2)}, u32[]{:S(2)}) collective-permute-start(f32[1,128,128]{2,1,0:T(8,128)S(1)} %constant_dynamic-slice_fusion), channel_id=1, source_target_pairs={{0,1},{1,0},{2,3},{3,2},{4,5},{5,4},{6,7},{7,6},{8,9},{9,8},{10,11... | collective-permute-start | bytes 196616 | tf_op jit(solution)/shard_map/ppermute | solution.py:164
  101.6 1.2 %collective-permute-done.3 = f32[1,128,128]{2,1,0:T(8,128)S(1)} collective-permute-done((f32[1,128,128]{2,1,0:T(8,128)S(1)}, f32[1,128,128]{2,1,0:T(8,128)S(1)}, u32[]{:S(2)}, u32[]{:S(2)}) %collective-permute-start.3) | collective-permute-done | bytes 65568 | tf_op jit(solution)/shard_map/ppermute | solution.py:164
  102.8 0.6 add_convert_fusion
  103.4 9.5 %all-to-all-done.3 = bf16[16,32,128]{2,1,0:T(8,128)(2,1)S(1)} async-done(((bf16[16,32,128]{2,1,0:T(8,128)(2,1)}), bf16[16,32,128]{2,1,0:T(8,128)(2,1)S(1)}, u32[]{:S(2)}, u32[]{:S(2)}) %all-to-all-start.3) | async-done | bytes 131104 | tf_op jit(solution)/shard_map/all_to_all | solution.py:155
  113.0 0.6 fusion.2
  (8 shorter events, 0.2 us)
Async XLA Ops:
  2.7 19.7 %copy-start = (bf16[1,128,128]{2,1,0:T(8,128)(2,1)S(1)}, bf16[1,128,128]{2,1,0:T(8,128)(2,1)}, u32[]{:S(2)}) copy-start(bf16[1,128,128]{2,1,0:T(8,128)(2,1)} %param.5) | copy-start | bytes 98308
  2.7 34.6 %all-to-all-start = ((bf16[16,40,128]{2,1,0:T(8,128)(2,1)}), bf16[16,40,128]{2,1,0:T(8,128)(2,1)S(1)}, u32[]{:S(2)}, u32[]{:S(2)}) async-start(bf16[16,40,128]{2,1,0:T(8,128)(2,1)} %broadcast_in_dim.14), calls=%async_computation | async-start | bytes 327680 | tf_op jit(solution)/shard_map/all_to_all | solution.py:155
  38.2 21.6 %all-to-all-start.1 = ((bf16[8,2,136,128]{3,2,1,0:T(8,128)(2,1)}), bf16[8,2,136,128]{3,2,1,0:T(8,128)(2,1)S(1)}, u32[]{:S(2)}, u32[]{:S(2)}) async-start(bf16[8,2,136,128]{3,2,1,0:T(8,128)(2,1)} %broadcast_in_dim.16), calls=%async_computation.1 | async-start | bytes 1114112 | tf_op jit(solution)/shard_map/all_to_all | solution.py:155
  68.8 9.7 %collective-permute-start = (bf16[8,128,128]{2,1,0:T(8,128)(2,1)S(1)}, bf16[8,128,128]{2,1,0:T(8,128)(2,1)S(1)}, u32[]{:S(2)}, u32[]{:S(2)}) collective-permute-start(bf16[8,128,128]{2,1,0:T(8,128)(2,1)S(1)} %get-tuple-element.14), channel_id=1, source_target_pairs={{0,64},{64,0},{128,192},{192,128},{256,320},{320,256},{384,448},{4... | collective-permute-start | bytes 786440 | tf_op jit(solution)/shard_map/ppermute | solution.py:164
  71.8 11.1 %all-to-all-start.2 = ((bf16[4,16,32,128]{3,2,1,0:T(8,128)(2,1)}), bf16[4,16,32,128]{3,2,1,0:T(8,128)(2,1)S(1)}, u32[]{:S(2)}, u32[]{:S(2)}) async-start(bf16[4,16,32,128]{3,2,1,0:T(8,128)(2,1)} %bitcast.4), calls=%async_computation.2 | async-start | bytes 1048576 | tf_op jit(solution)/shard_map/all_to_all | solution.py:155
  78.5 10.6 %collective-permute-start.1 = (bf16[4,128,128]{2,1,0:T(8,128)(2,1)S(1)}, bf16[4,128,128]{2,1,0:T(8,128)(2,1)S(1)}, u32[]{:S(2)}, u32[]{:S(2)}) collective-permute-start(bf16[4,128,128]{2,1,0:T(8,128)(2,1)S(1)} %fusion), channel_id=1, source_target_pairs={{0,128},{64,192},{128,0},{192,64},{256,384},{320,448},{384,256},{4... | collective-permute-start | bytes 393224 | tf_op jit(solution)/shard_map/ppermute | solution.py:164
  89.2 10.4 %collective-permute-start.2 = (bf16[2,128,128]{2,1,0:T(8,128)(2,1)S(1)}, bf16[2,128,128]{2,1,0:T(8,128)(2,1)S(1)}, u32[]{:S(2)}, u32[]{:S(2)}) collective-permute-start(bf16[2,128,128]{2,1,0:T(8,128)(2,1)S(1)} %fusion.1), channel_id=1, source_target_pairs={{0,256},{64,320},{128,384},{192,448},{256,0},{320,64},{384,128},{4... | collective-permute-start | bytes 196616 | tf_op jit(solution)/shard_map/ppermute | solution.py:164
  95.2 17.8 %all-to-all-start.3 = ((bf16[16,32,128]{2,1,0:T(8,128)(2,1)}), bf16[16,32,128]{2,1,0:T(8,128)(2,1)S(1)}, u32[]{:S(2)}, u32[]{:S(2)}) async-start(bf16[16,32,128]{2,1,0:T(8,128)(2,1)} %reduce_sum.21), calls=%async_computation.3 | async-start | bytes 262144 | tf_op jit(solution)/shard_map/all_to_all | solution.py:155
  99.7 3.1 %collective-permute-start.3 = (f32[1,128,128]{2,1,0:T(8,128)S(1)}, f32[1,128,128]{2,1,0:T(8,128)S(1)}, u32[]{:S(2)}, u32[]{:S(2)}) collective-permute-start(f32[1,128,128]{2,1,0:T(8,128)S(1)} %constant_dynamic-slice_fusion), channel_id=1, source_target_pairs={{0,1},{1,0},{2,3},{3,2},{4,5},{5,4},{6,7},{7,6},{8,9},{9,8},{10,11... | collective-permute-start | bytes 196616 | tf_op jit(solution)/shard_map/ppermute | solution.py:164

commit v7 on v6

--- a/solution.py
+++ b/solution.py
@@ -91,11 +91,9 @@
     own_scale = jnp.sum(mine_ref[...], axis=0, keepdims=True)
     coef = (lift_ref[own_block, own_vid] * own_scale).astype(jnp.bfloat16)
     total_ref[pl.ds(own_vid * v_len, v_len), :] += jnp.dot(coef, queries_of(own_block), preferred_element_type=jnp.float32)
-    bit = lax.axis_index("y") & 1
-    y_half = lax.axis_size("y") // 2
+    core = lax.axis_index("core")
     for pair in range(vid_rows // 2):
-        core, high = divmod(pair, y_half)
-        kept_at, sent_at = (4 * high + 2 * bit + core) * v_len, (4 * high + 2 - 2 * bit + core) * v_len
+        kept_at, sent_at = (2 * pair + core) * v_len, (2 * pair + 1 - core) * v_len
         dv_kept_ref[pair] = total_ref[pl.ds(pl.multiple_of(kept_at, v_len), v_len), :]
         dv_sent_ref[pair] = total_ref[pl.ds(pl.multiple_of(sent_at, v_len), v_len), :].astype(dv_sent_ref.dtype)
     total_ref[pl.ds(0, lanes), :] = lax.dot_general(
@@ -164,10 +162,10 @@
     return kept + lax.ppermute(sent, axis, across).astype(jnp.float32)
 
 
-def sum_over_bit(kept, axis, bit, dtype):
+def sum_over_bit(kept, axis, bit):
     kept = kept.reshape(-1, 2, *kept.shape[1:])
     own = (lax.axis_index(axis) >> bit) & 1
-    sent = lax.dynamic_index_in_dim(kept, 1 - own, 1, keepdims=False).astype(dtype)
+    sent = lax.dynamic_index_in_dim(kept, 1 - own, 1, keepdims=False).astype(jnp.bfloat16)
     return halve(lax.dynamic_index_in_dim(kept, own, 1, keepdims=False), sent, axis, bit)
 
 
@@ -182,13 +180,12 @@
     caps = lax.all_gather(caps, "x", axis=0, tiled=True)
     dq, own_dq, dv_kept, dv_sent = pair_grads(caps, vids, q_len, v_len)
     dq = sum_over(dq.reshape(x_count, z_count, q_len, features), "x").astype(jnp.bfloat16)
-    dv = halve(dv_kept, dv_sent, "y", 0)
+    dv = halve(dv_kept, dv_sent, "core", 0)
     last = lax.axis_size("y").bit_length() - 2
-    for bit in range(1, last):
-        dv = sum_over_bit(dv, "y", bit, jnp.bfloat16)
+    for bit in range(last):
+        dv = sum_over_bit(dv, "y", bit)
     dq, dv = lax.optimization_barrier((dq, dv))
-    dv = sum_over_bit(dv, "y", last, jnp.bfloat16)
-    dv = sum_over_bit(dv, "core", 0, jnp.float32)[0].astype(jnp.bfloat16)
+    dv = sum_over_bit(dv, "y", last)[0].astype(jnp.bfloat16)
     dq = (sum_over(dq, Z) + own_dq).astype(jnp.bfloat16)
     return dq[None], dv[None]
 

time: 114 us -> 112 us (0.982)
  the two profiles are of different devices: /device:TPU:2 before, /device:TPU:8 now
where the time goes in v7:
time: 112 us; the launch traced here: 111 us
  starting transfers between devices  51.1 us (46%)
  waiting for transfers between devices  28.9 us (26%)
  blocking collectives  15.7 us (14%)
  Pallas kernels  9 us (8%)
  local copies, waits for them, and re-layouts  2.32 us (2%)
  other arithmetic  2.08 us (2%)
  between operations  2.07 us (2%)
    all_to_all x4, starting transfers between devices, send(): return lax.all_to_all(parts, axis, 0, 0, tiled=True)  38.9 us
    all_to_all x4, waiting for transfers between devices, send(): return lax.all_to_all(parts, axis, 0, 0, tiled=True)  20.4 us
    all_gather x1, blocking collectives, local(): caps = lax.all_gather(caps, 'x', axis=0, tiled=True)  13.9 us
    ppermute x4, starting transfers between devices, halve(): return kept + lax.ppermute(sent, axis, across).astype(jnp.float32)  12.3 us
    pallas_call x1, Pallas kernels, pair_grads(): pl.pallas_call(functools.partial(pair_kernel, q_len=q_len, v_len=v_len, l...  9 us
    ppermute x4, waiting for transfers between devices, halve(): return kept + lax.ppermute(sent, axis, across).astype(jnp.float32)  8.55 us
    broadcast_in_dim x3, local copies, waits for them, and re-layouts, copies(): return jnp.broadcast_to(block[None], (count, *block.shape))  2.25 us
  transfers between devices with their start and end apart: 8, of which 6 were waited for; matrix products, arithmetic and copies ran while one was open for 1% of the time, Pallas kernels for 0%

profile of v7, /device:TPU:8, one launch (start us, length us, event | category | flops | bytes accessed | tf_op | source)
XLA Modules:
  0.0 111.3 jit_solution(10288795604031118314)
XLA Ops:
  1.3 0.7 pad_bitcast_fusion
  2.0 0.7 broadcast_in_dim.14
  2.7 0.0 copy-start
  2.7 19.0 %all-to-all-start = ((bf16[16,40,128]{2,1,0:T(8,128)(2,1)}), bf16[16,40,128]{2,1,0:T(8,128)(2,1)S(1)}, u32[]{:S(2)}, u32[]{:S(2)}) async-start(bf16[16,40,128]{2,1,0:T(8,128)(2,1)} %broadcast_in_dim.14), calls=%async_computation | async-start | bytes 327680 | tf_op jit(solution)/shard_map/all_to_all | solution.py:153
  22.3 0.0 copy-done
  22.3 1.9 %all_gather.6 = bf16[2,136,128]{2,1,0:T(8,128)(2,1)S(1)} all-gather(bf16[1,136,128]{2,1,0:T(8,128)(2,1)S(1)} %concatenate.7), channel_id=1, replica_groups=mesh['z_hi'=2,'y'=8,'x'=4,'z_lo'=8,'core'=2] {'core'}, dimensions={0}, use_global_device_ids=true | all-gather | bytes 104448 | tf_op jit(solution)/shard_map/all_gather | solution.py:176
  24.2 13.1 %all-to-all-done = bf16[16,40,128]{2,1,0:T(8,128)(2,1)S(1)} async-done(((bf16[16,40,128]{2,1,0:T(8,128)(2,1)}), bf16[16,40,128]{2,1,0:T(8,128)(2,1)S(1)}, u32[]{:S(2)}, u32[]{:S(2)}) %all-to-all-start) | async-done | bytes 163872 | tf_op jit(solution)/shard_map/all_to_all | solution.py:153
  37.3 0.9 broadcast_in_dim.16
  38.2 7.5 %all-to-all-start.1 = ((bf16[8,2,136,128]{3,2,1,0:T(8,128)(2,1)}), bf16[8,2,136,128]{3,2,1,0:T(8,128)(2,1)S(1)}, u32[]{:S(2)}, u32[]{:S(2)}) async-start(bf16[8,2,136,128]{3,2,1,0:T(8,128)(2,1)} %broadcast_in_dim.16), calls=%async_computation.1 | async-start | bytes 1114112 | tf_op jit(solution)/shard_map/all_to_all | solution.py:153
  45.7 13.9 %all_gather.7.caps_ref = bf16[64,40,128]{2,1,0:T(8,128)(2,1)S(1)} all-gather(bf16[16,40,128]{2,1,0:T(8,128)(2,1)S(1)} %all-to-all-done), channel_id=1, replica_groups=mesh['z_hi'=2,'y'=8,'x'=4,'z_lo'=8,'core'=2] {'x'}, dimensions={0}, use_global_device_ids=true | all-gather | bytes 819200 | tf_op jit(solution)/shard_map/all_gather | solution.py:180
  59.6 0.0 all-to-all-done.1
  59.6 9.0 %shard_map.59 = (bf16[64,32,128]{2,1,0:T(8,128)(2,1)}, f32[32,128]{1,0:T(8,128)S(1)}, f32[8,128,128]{2,1,0:T(8,128)S(1)}, bf16[8,128,128]{2,1,0:T(8,128)(2,1)S(1)}) custom-call(bf16[64,40,128]{2,1,0:T(8,128)(2,1)S(1)} %all_gather.7.caps_ref, bf16[16,136,128]{2,1,0:T(8,128)(2,1)S(1)} %bitcast.24), custom_call_target="tpu_custom_call" | custom-call | flops 3221225472 | bytes 2097152 | tf_op jit(solution)/shard_map/pallas_call | solution.py:108
  68.6 1.9 %collective-permute-start = (bf16[8,128,128]{2,1,0:T(8,128)(2,1)S(1)}, bf16[8,128,128]{2,1,0:T(8,128)(2,1)S(1)}, u32[]{:S(2)}, u32[]{:S(2)}) collective-permute-start(bf16[8,128,128]{2,1,0:T(8,128)(2,1)S(1)} %get-tuple-element.14), channel_id=1, source_target_pairs={{0,1},{1,0},{2,3},{3,2},{4,5},{5,4},{6,7},{7,6},{8,9},{9,8},{10,11... | collective-permute-start | bytes 786440 | tf_op jit(solution)/shard_map/ppermute | solution.py:162
  70.5 1.5 %collective-permute-done = bf16[8,128,128]{2,1,0:T(8,128)(2,1)S(1)} collective-permute-done((bf16[8,128,128]{2,1,0:T(8,128)(2,1)S(1)}, bf16[8,128,128]{2,1,0:T(8,128)(2,1)S(1)}, u32[]{:S(2)}, u32[]{:S(2)}) %collective-permute-start) | collective-permute-done | bytes 262176 | tf_op jit(solution)/shard_map/ppermute | solution.py:162
  72.1 2.5 %collective-permute-start.1 = (bf16[4,128,128]{2,1,0:T(8,128)(2,1)S(1)}, bf16[4,128,128]{2,1,0:T(8,128)(2,1)S(1)}, u32[]{:S(2)}, u32[]{:S(2)}) collective-permute-start(bf16[4,128,128]{2,1,0:T(8,128)(2,1)S(1)} %fusion), channel_id=1, source_target_pairs={{0,64},{64,0},{128,192},{192,128},{256,320},{320,256},{384,448},{4... | collective-permute-start | bytes 393224 | tf_op jit(solution)/shard_map/ppermute | solution.py:162
  74.7 4.3 %all-to-all-start.2 = ((bf16[4,16,32,128]{3,2,1,0:T(8,128)(2,1)}), bf16[4,16,32,128]{3,2,1,0:T(8,128)(2,1)S(1)}, u32[]{:S(2)}, u32[]{:S(2)}) async-start(bf16[4,16,32,128]{3,2,1,0:T(8,128)(2,1)} %bitcast.4), calls=%async_computation.2 | async-start | bytes 1048576 | tf_op jit(solution)/shard_map/all_to_all | solution.py:153
  79.0 0.6 collective-permute-done.1
  79.6 4.6 %collective-permute-start.2 = (bf16[2,128,128]{2,1,0:T(8,128)(2,1)S(1)}, bf16[2,128,128]{2,1,0:T(8,128)(2,1)S(1)}, u32[]{:S(2)}, u32[]{:S(2)}) collective-permute-start(bf16[2,128,128]{2,1,0:T(8,128)(2,1)S(1)} %fusion.1), channel_id=1, source_target_pairs={{0,128},{64,192},{128,0},{192,64},{256,384},{320,448},{384,256},{4... | collective-permute-start | bytes 196616 | tf_op jit(solution)/shard_map/ppermute | solution.py:162
  84.2 4.3 %all-to-all-done.2 = bf16[4,16,32,128]{3,2,1,0:T(8,128)(2,1)S(1)} async-done(((bf16[4,16,32,128]{3,2,1,0:T(8,128)(2,1)}), bf16[4,16,32,128]{3,2,1,0:T(8,128)(2,1)S(1)}, u32[]{:S(2)}, u32[]{:S(2)}) %all-to-all-start.2) | async-done | bytes 524320 | tf_op jit(solution)/shard_map/all_to_all | solution.py:153
  88.5 0.7 reduce_sum.21
  89.2 0.0 collective-permute-done.2
  89.2 8.0 %all-to-all-start.3 = ((bf16[16,32,128]{2,1,0:T(8,128)(2,1)}), bf16[16,32,128]{2,1,0:T(8,128)(2,1)S(1)}, u32[]{:S(2)}, u32[]{:S(2)}) async-start(bf16[16,32,128]{2,1,0:T(8,128)(2,1)} %reduce_sum.21), calls=%async_computation.3 | async-start | bytes 262144 | tf_op jit(solution)/shard_map/all_to_all | solution.py:153
  97.3 3.2 %collective-permute-start.3 = (bf16[1,128,128]{2,1,0:T(8,128)(2,1)S(1)}, bf16[1,128,128]{2,1,0:T(8,128)(2,1)S(1)}, u32[]{:S(2)}, u32[]{:S(2)}) collective-permute-start(bf16[1,128,128]{2,1,0:T(8,128)(2,1)S(1)} %dynamic-slice_convert_fusion.1), channel_id=1, source_target_pairs={{0,256},{64,320},{128,384},{192,448},{256,0},{320,64},{384,128},{4... | collective-permute-start | bytes 98312 | tf_op jit(solution)/shard_map/ppermute | solution.py:162
  100.5 6.5 %collective-permute-done.3 = bf16[1,128,128]{2,1,0:T(8,128)(2,1)S(1)} collective-permute-done((bf16[1,128,128]{2,1,0:T(8,128)(2,1)S(1)}, bf16[1,128,128]{2,1,0:T(8,128)(2,1)S(1)}, u32[]{:S(2)}, u32[]{:S(2)}) %collective-permute-start.3) | collective-permute-done | bytes 32800 | tf_op jit(solution)/shard_map/ppermute | solution.py:162
  107.0 0.6 add_convert_fusion
  107.6 3.0 %all-to-all-done.3 = bf16[16,32,128]{2,1,0:T(8,128)(2,1)S(1)} async-done(((bf16[16,32,128]{2,1,0:T(8,128)(2,1)}), bf16[16,32,128]{2,1,0:T(8,128)(2,1)S(1)}, u32[]{:S(2)}, u32[]{:S(2)}) %all-to-all-start.3) | async-done | bytes 131104 | tf_op jit(solution)/shard_map/all_to_all | solution.py:153
  110.6 0.6 fusion.2
  (8 shorter events, 0.2 us)
Async XLA Ops:
  2.7 19.7 %copy-start = (bf16[1,128,128]{2,1,0:T(8,128)(2,1)S(1)}, bf16[1,128,128]{2,1,0:T(8,128)(2,1)}, u32[]{:S(2)}) copy-start(bf16[1,128,128]{2,1,0:T(8,128)(2,1)} %param.5) | copy-start | bytes 98308
  2.7 34.6 %all-to-all-start = ((bf16[16,40,128]{2,1,0:T(8,128)(2,1)}), bf16[16,40,128]{2,1,0:T(8,128)(2,1)S(1)}, u32[]{:S(2)}, u32[]{:S(2)}) async-start(bf16[16,40,128]{2,1,0:T(8,128)(2,1)} %broadcast_in_dim.14), calls=%async_computation | async-start | bytes 327680 | tf_op jit(solution)/shard_map/all_to_all | solution.py:153
  38.2 21.4 %all-to-all-start.1 = ((bf16[8,2,136,128]{3,2,1,0:T(8,128)(2,1)}), bf16[8,2,136,128]{3,2,1,0:T(8,128)(2,1)S(1)}, u32[]{:S(2)}, u32[]{:S(2)}) async-start(bf16[8,2,136,128]{3,2,1,0:T(8,128)(2,1)} %broadcast_in_dim.16), calls=%async_computation.1 | async-start | bytes 1114112 | tf_op jit(solution)/shard_map/all_to_all | solution.py:153
  68.6 3.4 %collective-permute-start = (bf16[8,128,128]{2,1,0:T(8,128)(2,1)S(1)}, bf16[8,128,128]{2,1,0:T(8,128)(2,1)S(1)}, u32[]{:S(2)}, u32[]{:S(2)}) collective-permute-start(bf16[8,128,128]{2,1,0:T(8,128)(2,1)S(1)} %get-tuple-element.14), channel_id=1, source_target_pairs={{0,1},{1,0},{2,3},{3,2},{4,5},{5,4},{6,7},{7,6},{8,9},{9,8},{10,11... | collective-permute-start | bytes 786440 | tf_op jit(solution)/shard_map/ppermute | solution.py:162
  72.1 7.4 %collective-permute-start.1 = (bf16[4,128,128]{2,1,0:T(8,128)(2,1)S(1)}, bf16[4,128,128]{2,1,0:T(8,128)(2,1)S(1)}, u32[]{:S(2)}, u32[]{:S(2)}) collective-permute-start(bf16[4,128,128]{2,1,0:T(8,128)(2,1)S(1)} %fusion), channel_id=1, source_target_pairs={{0,64},{64,0},{128,192},{192,128},{256,320},{320,256},{384,448},{4... | collective-permute-start | bytes 393224 | tf_op jit(solution)/shard_map/ppermute | solution.py:162
  74.7 13.8 %all-to-all-start.2 = ((bf16[4,16,32,128]{3,2,1,0:T(8,128)(2,1)}), bf16[4,16,32,128]{3,2,1,0:T(8,128)(2,1)S(1)}, u32[]{:S(2)}, u32[]{:S(2)}) async-start(bf16[4,16,32,128]{3,2,1,0:T(8,128)(2,1)} %bitcast.4), calls=%async_computation.2 | async-start | bytes 1048576 | tf_op jit(solution)/shard_map/all_to_all | solution.py:153
  79.6 9.6 %collective-permute-start.2 = (bf16[2,128,128]{2,1,0:T(8,128)(2,1)S(1)}, bf16[2,128,128]{2,1,0:T(8,128)(2,1)S(1)}, u32[]{:S(2)}, u32[]{:S(2)}) collective-permute-start(bf16[2,128,128]{2,1,0:T(8,128)(2,1)S(1)} %fusion.1), channel_id=1, source_target_pairs={{0,128},{64,192},{128,0},{192,64},{256,384},{320,448},{384,256},{4... | collective-permute-start | bytes 196616 | tf_op jit(solution)/shard_map/ppermute | solution.py:162
  89.2 21.4 %all-to-all-start.3 = ((bf16[16,32,128]{2,1,0:T(8,128)(2,1)}), bf16[16,32,128]{2,1,0:T(8,128)(2,1)S(1)}, u32[]{:S(2)}, u32[]{:S(2)}) async-start(bf16[16,32,128]{2,1,0:T(8,128)(2,1)} %reduce_sum.21), calls=%async_computation.3 | async-start | bytes 262144 | tf_op jit(solution)/shard_map/all_to_all | solution.py:153
  97.3 9.7 %collective-permute-start.3 = (bf16[1,128,128]{2,1,0:T(8,128)(2,1)S(1)}, bf16[1,128,128]{2,1,0:T(8,128)(2,1)S(1)}, u32[]{:S(2)}, u32[]{:S(2)}) collective-permute-start(bf16[1,128,128]{2,1,0:T(8,128)(2,1)S(1)} %dynamic-slice_convert_fusion.1), channel_id=1, source_target_pairs={{0,256},{64,320},{128,384},{192,448},{256,0},{320,64},{384,128},{4... | collective-permute-start | bytes 98312 | tf_op jit(solution)/shard_map/ppermute | solution.py:162

commit v8 on v7

--- a/solution.py
+++ b/solution.py
@@ -91,9 +91,10 @@
     own_scale = jnp.sum(mine_ref[...], axis=0, keepdims=True)
     coef = (lift_ref[own_block, own_vid] * own_scale).astype(jnp.bfloat16)
     total_ref[pl.ds(own_vid * v_len, v_len), :] += jnp.dot(coef, queries_of(own_block), preferred_element_type=jnp.float32)
-    core = lax.axis_index("core")
+    bit = lax.axis_index("y") & 1
     for pair in range(vid_rows // 2):
-        kept_at, sent_at = (2 * pair + core) * v_len, (2 * pair + 1 - core) * v_len
+        high, core = divmod(pair, 2)
+        kept_at, sent_at = (4 * high + 2 * bit + core) * v_len, (4 * high + 2 - 2 * bit + core) * v_len
         dv_kept_ref[pair] = total_ref[pl.ds(pl.multiple_of(kept_at, v_len), v_len), :]
         dv_sent_ref[pair] = total_ref[pl.ds(pl.multiple_of(sent_at, v_len), v_len), :].astype(dv_sent_ref.dtype)
     total_ref[pl.ds(0, lanes), :] = lax.dot_general(
@@ -180,9 +181,10 @@
     caps = lax.all_gather(caps, "x", axis=0, tiled=True)
     dq, own_dq, dv_kept, dv_sent = pair_grads(caps, vids, q_len, v_len)
     dq = sum_over(dq.reshape(x_count, z_count, q_len, features), "x").astype(jnp.bfloat16)
-    dv = halve(dv_kept, dv_sent, "core", 0)
+    dv = halve(dv_kept, dv_sent, "y", 0)
+    dv = sum_over_bit(dv, "core", 0)
     last = lax.axis_size("y").bit_length() - 2
-    for bit in range(last):
+    for bit in range(1, last):
         dv = sum_over_bit(dv, "y", bit)
     dq, dv = lax.optimization_barrier((dq, dv))
     dv = sum_over_bit(dv, "y", last)[0].astype(jnp.bfloat16)

time: 112 us -> 119 us (1.062)
  the two profiles are of different devices: /device:TPU:8 before, /device:TPU:2 now
where the time goes in v8:
time: 119 us; the launch traced here: 118 us
  starting transfers between devices  51.4 us (43%)
  waiting for transfers between devices  35.4 us (30%)
  blocking collectives  15.7 us (13%)
  Pallas kernels  9.01 us (8%)
  local copies, waits for them, and re-layouts  2.32 us (2%)
  other arithmetic  2.08 us (2%)
  between operations  2.07 us (2%)
    all_to_all x4, starting transfers between devices, send(): return lax.all_to_all(parts, axis, 0, 0, tiled=True)  40.8 us
    all_to_all x4, waiting for transfers between devices, send(): return lax.all_to_all(parts, axis, 0, 0, tiled=True)  22.4 us
    all_gather x1, blocking collectives, local(): caps = lax.all_gather(caps, 'x', axis=0, tiled=True)  13.9 us
    ppermute x4, waiting for transfers between devices, halve(): return kept + lax.ppermute(sent, axis, across).astype(jnp.float32)  13 us
    ppermute x4, starting transfers between devices, halve(): return kept + lax.ppermute(sent, axis, across).astype(jnp.float32)  10.6 us
    pallas_call x1, Pallas kernels, pair_grads(): pl.pallas_call(functools.partial(pair_kernel, q_len=q_len, v_len=v_len, l...  9.01 us
  transfers between devices with their start and end apart: 8, of which 6 were waited for; matrix products, arithmetic and copies ran while one was open for 1% of the time, Pallas kernels for 0%

profile of v8, /device:TPU:2, one launch (start us, length us, event | category | flops | bytes accessed | tf_op | source)
XLA Modules:
  0.0 118.0 jit_solution(18114312733175746548)
XLA Ops:
  1.3 0.7 pad_bitcast_fusion
  2.0 0.7 broadcast_in_dim.14
  2.7 0.0 copy-start
  2.7 19.0 %all-to-all-start = ((bf16[16,40,128]{2,1,0:T(8,128)(2,1)}), bf16[16,40,128]{2,1,0:T(8,128)(2,1)S(1)}, u32[]{:S(2)}, u32[]{:S(2)}) async-start(bf16[16,40,128]{2,1,0:T(8,128)(2,1)} %broadcast_in_dim.14), calls=%async_computation | async-start | bytes 327680 | tf_op jit(solution)/shard_map/all_to_all | solution.py:154
  22.3 0.0 copy-done
  22.3 1.9 %all_gather.6 = bf16[2,136,128]{2,1,0:T(8,128)(2,1)S(1)} all-gather(bf16[1,136,128]{2,1,0:T(8,128)(2,1)S(1)} %concatenate.7), channel_id=1, replica_groups=mesh['z_hi'=2,'y'=8,'x'=4,'z_lo'=8,'core'=2] {'core'}, dimensions={0}, use_global_device_ids=true | all-gather | bytes 104448 | tf_op jit(solution)/shard_map/all_gather | solution.py:177
  24.2 13.1 %all-to-all-done = bf16[16,40,128]{2,1,0:T(8,128)(2,1)S(1)} async-done(((bf16[16,40,128]{2,1,0:T(8,128)(2,1)}), bf16[16,40,128]{2,1,0:T(8,128)(2,1)S(1)}, u32[]{:S(2)}, u32[]{:S(2)}) %all-to-all-start) | async-done | bytes 163872 | tf_op jit(solution)/shard_map/all_to_all | solution.py:154
  37.3 0.9 broadcast_in_dim.16
  38.2 7.1 %all-to-all-start.1 = ((bf16[8,2,136,128]{3,2,1,0:T(8,128)(2,1)}), bf16[8,2,136,128]{3,2,1,0:T(8,128)(2,1)S(1)}, u32[]{:S(2)}, u32[]{:S(2)}) async-start(bf16[8,2,136,128]{3,2,1,0:T(8,128)(2,1)} %broadcast_in_dim.16), calls=%async_computation.1 | async-start | bytes 1114112 | tf_op jit(solution)/shard_map/all_to_all | solution.py:154
  45.3 13.9 %all_gather.7.caps_ref = bf16[64,40,128]{2,1,0:T(8,128)(2,1)S(1)} all-gather(bf16[16,40,128]{2,1,0:T(8,128)(2,1)S(1)} %all-to-all-done), channel_id=1, replica_groups=mesh['z_hi'=2,'y'=8,'x'=4,'z_lo'=8,'core'=2] {'x'}, dimensions={0}, use_global_device_ids=true | all-gather | bytes 819200 | tf_op jit(solution)/shard_map/all_gather | solution.py:181
  59.1 0.6 all-to-all-done.1
  59.8 9.0 %shard_map.59 = (bf16[64,32,128]{2,1,0:T(8,128)(2,1)}, f32[32,128]{1,0:T(8,128)S(1)}, f32[8,128,128]{2,1,0:T(8,128)S(1)}, bf16[8,128,128]{2,1,0:T(8,128)(2,1)S(1)}) custom-call(bf16[64,40,128]{2,1,0:T(8,128)(2,1)S(1)} %all_gather.7.caps_ref, bf16[16,136,128]{2,1,0:T(8,128)(2,1)S(1)} %bitcast.24), custom_call_target="tpu_custom_call" | custom-call | flops 3221225472 | bytes 2097152 | tf_op jit(solution)/shard_map/pallas_call | solution.py:109
  68.8 3.0 %collective-permute-start = (bf16[8,128,128]{2,1,0:T(8,128)(2,1)S(1)}, bf16[8,128,128]{2,1,0:T(8,128)(2,1)S(1)}, u32[]{:S(2)}, u32[]{:S(2)}) collective-permute-start(bf16[8,128,128]{2,1,0:T(8,128)(2,1)S(1)} %get-tuple-element.14), channel_id=1, source_target_pairs={{0,64},{64,0},{128,192},{192,128},{256,320},{320,256},{384,448},{4... | collective-permute-start | bytes 786440 | tf_op jit(solution)/shard_map/ppermute | solution.py:163
  71.8 5.2 %collective-permute-done = bf16[8,128,128]{2,1,0:T(8,128)(2,1)S(1)} collective-permute-done((bf16[8,128,128]{2,1,0:T(8,128)(2,1)S(1)}, bf16[8,128,128]{2,1,0:T(8,128)(2,1)S(1)}, u32[]{:S(2)}, u32[]{:S(2)}) %collective-permute-start) | collective-permute-done | bytes 262176 | tf_op jit(solution)/shard_map/ppermute | solution.py:163
  77.1 1.9 %collective-permute-start.1 = (bf16[4,128,128]{2,1,0:T(8,128)(2,1)S(1)}, bf16[4,128,128]{2,1,0:T(8,128)(2,1)S(1)}, u32[]{:S(2)}, u32[]{:S(2)}) collective-permute-start(bf16[4,128,128]{2,1,0:T(8,128)(2,1)S(1)} %fusion), channel_id=1, source_target_pairs={{0,1},{1,0},{2,3},{3,2},{4,5},{5,4},{6,7},{7,6},{8,9},{9,8},{10,11... | collective-permute-start | bytes 393224 | tf_op jit(solution)/shard_map/ppermute | solution.py:163
  79.1 4.8 %all-to-all-start.2 = ((bf16[4,16,32,128]{3,2,1,0:T(8,128)(2,1)}), bf16[4,16,32,128]{3,2,1,0:T(8,128)(2,1)S(1)}, u32[]{:S(2)}, u32[]{:S(2)}) async-start(bf16[4,16,32,128]{3,2,1,0:T(8,128)(2,1)} %bitcast.4), calls=%async_computation.2 | async-start | bytes 1048576 | tf_op jit(solution)/shard_map/all_to_all | solution.py:154
  83.9 0.0 collective-permute-done.1
  84.0 3.7 %collective-permute-start.2 = (bf16[2,128,128]{2,1,0:T(8,128)(2,1)S(1)}, bf16[2,128,128]{2,1,0:T(8,128)(2,1)S(1)}, u32[]{:S(2)}, u32[]{:S(2)}) collective-permute-start(bf16[2,128,128]{2,1,0:T(8,128)(2,1)S(1)} %fusion.1), channel_id=1, source_target_pairs={{0,128},{64,192},{128,0},{192,64},{256,384},{320,448},{384,256},{4... | collective-permute-start | bytes 196616 | tf_op jit(solution)/shard_map/ppermute | solution.py:163
  87.7 4.9 %all-to-all-done.2 = bf16[4,16,32,128]{3,2,1,0:T(8,128)(2,1)S(1)} async-done(((bf16[4,16,32,128]{3,2,1,0:T(8,128)(2,1)}), bf16[4,16,32,128]{3,2,1,0:T(8,128)(2,1)S(1)}, u32[]{:S(2)}, u32[]{:S(2)}) %all-to-all-start.2) | async-done | bytes 524320 | tf_op jit(solution)/shard_map/all_to_all | solution.py:154
  92.6 0.7 reduce_sum.21
  93.3 0.0 collective-permute-done.2
  93.4 9.9 %all-to-all-start.3 = ((bf16[16,32,128]{2,1,0:T(8,128)(2,1)}), bf16[16,32,128]{2,1,0:T(8,128)(2,1)S(1)}, u32[]{:S(2)}, u32[]{:S(2)}) async-start(bf16[16,32,128]{2,1,0:T(8,128)(2,1)} %reduce_sum.21), calls=%async_computation.3 | async-start | bytes 262144 | tf_op jit(solution)/shard_map/all_to_all | solution.py:154
  103.3 1.9 %collective-permute-start.3 = (bf16[1,128,128]{2,1,0:T(8,128)(2,1)S(1)}, bf16[1,128,128]{2,1,0:T(8,128)(2,1)S(1)}, u32[]{:S(2)}, u32[]{:S(2)}) collective-permute-start(bf16[1,128,128]{2,1,0:T(8,128)(2,1)S(1)} %dynamic-slice_convert_fusion.1), channel_id=1, source_target_pairs={{0,256},{64,320},{128,384},{192,448},{256,0},{320,64},{384,128},{4... | collective-permute-start | bytes 98312 | tf_op jit(solution)/shard_map/ppermute | solution.py:163
  105.2 7.8 %collective-permute-done.3 = bf16[1,128,128]{2,1,0:T(8,128)(2,1)S(1)} collective-permute-done((bf16[1,128,128]{2,1,0:T(8,128)(2,1)S(1)}, bf16[1,128,128]{2,1,0:T(8,128)(2,1)S(1)}, u32[]{:S(2)}, u32[]{:S(2)}) %collective-permute-start.3) | collective-permute-done | bytes 32800 | tf_op jit(solution)/shard_map/ppermute | solution.py:163
  113.0 0.6 add_convert_fusion
  113.6 3.8 %all-to-all-done.3 = bf16[16,32,128]{2,1,0:T(8,128)(2,1)S(1)} async-done(((bf16[16,32,128]{2,1,0:T(8,128)(2,1)}), bf16[16,32,128]{2,1,0:T(8,128)(2,1)S(1)}, u32[]{:S(2)}, u32[]{:S(2)}) %all-to-all-start.3) | async-done | bytes 131104 | tf_op jit(solution)/shard_map/all_to_all | solution.py:154
  117.4 0.6 fusion.2
  (8 shorter events, 0.2 us)
Async XLA Ops:
  2.7 19.7 %copy-start = (bf16[1,128,128]{2,1,0:T(8,128)(2,1)S(1)}, bf16[1,128,128]{2,1,0:T(8,128)(2,1)}, u32[]{:S(2)}) copy-start(bf16[1,128,128]{2,1,0:T(8,128)(2,1)} %param.5) | copy-start | bytes 98308
  2.7 34.6 %all-to-all-start = ((bf16[16,40,128]{2,1,0:T(8,128)(2,1)}), bf16[16,40,128]{2,1,0:T(8,128)(2,1)S(1)}, u32[]{:S(2)}, u32[]{:S(2)}) async-start(bf16[16,40,128]{2,1,0:T(8,128)(2,1)} %broadcast_in_dim.14), calls=%async_computation | async-start | bytes 327680 | tf_op jit(solution)/shard_map/all_to_all | solution.py:154
  38.2 21.6 %all-to-all-start.1 = ((bf16[8,2,136,128]{3,2,1,0:T(8,128)(2,1)}), bf16[8,2,136,128]{3,2,1,0:T(8,128)(2,1)S(1)}, u32[]{:S(2)}, u32[]{:S(2)}) async-start(bf16[8,2,136,128]{3,2,1,0:T(8,128)(2,1)} %broadcast_in_dim.16), calls=%async_computation.1 | async-start | bytes 1114112 | tf_op jit(solution)/shard_map/all_to_all | solution.py:154
  68.8 8.3 %collective-permute-start = (bf16[8,128,128]{2,1,0:T(8,128)(2,1)S(1)}, bf16[8,128,128]{2,1,0:T(8,128)(2,1)S(1)}, u32[]{:S(2)}, u32[]{:S(2)}) collective-permute-start(bf16[8,128,128]{2,1,0:T(8,128)(2,1)S(1)} %get-tuple-element.14), channel_id=1, source_target_pairs={{0,64},{64,0},{128,192},{192,128},{256,320},{320,256},{384,448},{4... | collective-permute-start | bytes 786440 | tf_op jit(solution)/shard_map/ppermute | solution.py:163
  77.1 6.8 %collective-permute-start.1 = (bf16[4,128,128]{2,1,0:T(8,128)(2,1)S(1)}, bf16[4,128,128]{2,1,0:T(8,128)(2,1)S(1)}, u32[]{:S(2)}, u32[]{:S(2)}) collective-permute-start(bf16[4,128,128]{2,1,0:T(8,128)(2,1)S(1)} %fusion), channel_id=1, source_target_pairs={{0,1},{1,0},{2,3},{3,2},{4,5},{5,4},{6,7},{7,6},{8,9},{9,8},{10,11... | collective-permute-start | bytes 393224 | tf_op jit(solution)/shard_map/ppermute | solution.py:163
  79.1 13.5 %all-to-all-start.2 = ((bf16[4,16,32,128]{3,2,1,0:T(8,128)(2,1)}), bf16[4,16,32,128]{3,2,1,0:T(8,128)(2,1)S(1)}, u32[]{:S(2)}, u32[]{:S(2)}) async-start(bf16[4,16,32,128]{3,2,1,0:T(8,128)(2,1)} %bitcast.4), calls=%async_computation.2 | async-start | bytes 1048576 | tf_op jit(solution)/shard_map/all_to_all | solution.py:154
  84.0 9.4 %collective-permute-start.2 = (bf16[2,128,128]{2,1,0:T(8,128)(2,1)S(1)}, bf16[2,128,128]{2,1,0:T(8,128)(2,1)S(1)}, u32[]{:S(2)}, u32[]{:S(2)}) collective-permute-start(bf16[2,128,128]{2,1,0:T(8,128)(2,1)S(1)} %fusion.1), channel_id=1, source_target_pairs={{0,128},{64,192},{128,0},{192,64},{256,384},{320,448},{384,256},{4... | collective-permute-start | bytes 196616 | tf_op jit(solution)/shard_map/ppermute | solution.py:163
  93.4 24.0 %all-to-all-start.3 = ((bf16[16,32,128]{2,1,0:T(8,128)(2,1)}), bf16[16,32,128]{2,1,0:T(8,128)(2,1)S(1)}, u32[]{:S(2)}, u32[]{:S(2)}) async-start(bf16[16,32,128]{2,1,0:T(8,128)(2,1)} %reduce_sum.21), calls=%async_computation.3 | async-start | bytes 262144 | tf_op jit(solution)/shard_map/all_to_all | solution.py:154
  103.3 9.7 %collective-permute-start.3 = (bf16[1,128,128]{2,1,0:T(8,128)(2,1)S(1)}, bf16[1,128,128]{2,1,0:T(8,128)(2,1)S(1)}, u32[]{:S(2)}, u32[]{:S(2)}) collective-permute-start(bf16[1,128,128]{2,1,0:T(8,128)(2,1)S(1)} %dynamic-slice_convert_fusion.1), channel_id=1, source_target_pairs={{0,256},{64,320},{128,384},{192,448},{256,0},{320,64},{384,128},{4... | collective-permute-start | bytes 98312 | tf_op jit(solution)/shard_map/ppermute | solution.py:163
